TPU v7x, 32 devices: a whole 2x2x4 slice. The times are simulated.
32 devices in a mesh: dp: 8 (over z, y), row: 2 (over core), col: 2 (over x).
Axes of the slice: x: 2, y: 2, z: 4, core: 2. Of those that a mesh axis runs over, the one named last changes fastest.
Arguments:
- tokens: bfloat16 [8192, 1024], P(('dp', 'row'), 'col'), may hold values from -13 to 13
- cotangent: bfloat16 [8192, 1024], P(('dp', 'row'), 'col'), may hold values from -13 to 13
- input_projection_weight: float32 [1024, 3, 1024], P('col', None, 'row'), may hold values from -0.1875 to 0.1875
- conv_weight: float32 [3, 1024], P(None, 'row'), may hold values from -3 to 3
- output_projection_weight: float32 [1024, 1024], P('row', 'col'), may hold values from -0.1875 to 0.1875
- norm_gains: float32 [2, 1024], P(None, 'col'), may hold values from 0.5 to 1.5
- gate_up_weight: float32 [1024, 2, 4608], P('col', None, 'row'), may hold values from -0.21875 to 0.21875
- down_projection_weight: float32 [4608, 1024], P('row', 'col'), may hold values from -0.09375 to 0.09375
- in_first: float32 [1024, 3, 1024], P('col', None, 'row'), may hold values from -512 to 512
- in_second: float32 [1024, 3, 1024], P('col', None, 'row'), may hold values from 5464.064 to 21848.064
- conv_first: float32 [3, 1024], P(None, 'row'), may hold values from -512 to 512
- conv_second: float32 [3, 1024], P(None, 'row'), may hold values from 5464.064 to 21848.064
- out_first: float32 [1024, 1024], P('row', 'col'), may hold values from -512 to 512
- out_second: float32 [1024, 1024], P('row', 'col'), may hold values from 5464.064 to 21848.064
- gain_first: float32 [2, 1024], P(None, 'col'), may hold values from -640 to 640
- gain_second: float32 [2, 1024], P(None, 'col'), may hold values from 8192 to 32768
- gu_first: float32 [1024, 2, 4608], P('col', None, 'row'), may hold values from -160 to 160
- gu_second: float32 [1024, 2, 4608], P('col', None, 'row'), may hold values from 434.176 to 1744.896
- down_first: float32 [4608, 1024], P('row', 'col'), may hold values from -320 to 320
- down_second: float32 [4608, 1024], P('row', 'col'), may hold values from 1966.08 to 7864.32
Outputs:
- output: bfloat16 [8192, 1024], P(('dp', 'row'), 'col')
- token_grad: bfloat16 [8192, 1024], P(('dp', 'row'), 'col')
- in_weight_new: float32 [1024, 3, 1024], P('col', None, 'row')
- in_first_new: float32 [1024, 3, 1024], P('col', None, 'row')
- in_second_new: float32 [1024, 3, 1024], P('col', None, 'row')
- conv_weight_new: float32 [3, 1024], P(None, 'row')
- conv_first_new: float32 [3, 1024], P(None, 'row')
- conv_second_new: float32 [3, 1024], P(None, 'row')
- out_weight_new: float32 [1024, 1024], P('row', 'col')
- out_first_new: float32 [1024, 1024], P('row', 'col')
- out_second_new: float32 [1024, 1024], P('row', 'col')
- gains_new: float32 [2, 1024], P(None, 'col')
- gain_first_new: float32 [2, 1024], P(None, 'col')
- gain_second_new: float32 [2, 1024], P(None, 'col')
- gate_up_new: float32 [1024, 2, 4608], P('col', None, 'row')
- gu_first_new: float32 [1024, 2, 4608], P('col', None, 'row')
- gu_second_new: float32 [1024, 2, 4608], P('col', None, 'row')
- down_weight_new: float32 [4608, 1024], P('row', 'col')
- down_first_new: float32 [4608, 1024], P('row', 'col')
- down_second_new: float32 [4608, 1024], P('row', 'col')
- trust_norms: float32 [7, 2], replicated
All inputs are finite; a program needn't handle non-finite values.
Results may differ from a plain program's by a relative error of at most 0.013.
Values may be sent and summed in bfloat16 or wider, within the bound.
No kernel may reach another device: no remote copies, remote signals or barrier semaphores. Data moves between devices by JAX's collectives and lax.ppermute only.
A program may use at most 256 MiB of HBM per device.

v0:
```python
import functools

import jax
import jax.numpy as jnp
from jax import lax
from jax.experimental import pallas as pl
from jax.experimental.layout import Layout, with_layout_constraint
from jax.experimental.pallas import tpu as pltpu
from jax.sharding import PartitionSpec as P

D = 1024
SEQ_LEAST = 4096
STEP = 5
MIB = 1024 * 1024


norm_eps = 1e-05
adam_eps = 1e-06
beta_one = 0.5
beta_two = 0.6
learn_rate = 0.5
decay_rate = 0.01
low = jnp.bfloat16
wide = jnp.float32


def from_behind(block, axis, distance):
    devices = range(lax.axis_size(axis))
    route = [(i - distance, i) for i in devices if i - distance in devices]
    return lax.ppermute(block, axis, route)


def swap(values, axis):
    return lax.ppermute(values, axis, [(0, 1), (1, 0)])


def swap_halves(halves):
    return [swap(half, "row") for half in halves]


def to_home(values):
    return lax.ppermute(values, ("row", "col"), [(1, 0), (2, 3)])


def home_to_sibling(values):
    return lax.ppermute(values, ("row", "col"), [(0, 2), (3, 1)])


def home_to_away(values):
    return lax.ppermute(values, ("row", "col"), [(0, 1), (3, 2)])


def sibling_to_home(values):
    return lax.ppermute(values, ("row", "col"), [(2, 0), (1, 3)])


def contract(left, right, left_dim, right_dim):
    return lax.dot_general(
        left, right, (((left_dim,), (right_dim,)), ((), ())), preferred_element_type=wide
    )


def mul(left, right):
    return contract(left, right, 1, 0)


def mul_t(left, right):
    return contract(left, right, 1, 1)


def t_mul(left, right):
    return contract(left, right, 0, 0)


def lamb_moments(weight, grad, first, second, decay):
    first_new = beta_one * first + (1.0 - beta_one) * grad
    second_new = beta_two * second + (1.0 - beta_two) * grad * grad
    direction = (first_new * (1.0 / (1.0 - beta_one**STEP))) / (
        jnp.sqrt(second_new * (1.0 / (1.0 - beta_two**STEP))) + adam_eps
    ) + decay * weight
    return (first_new, second_new, direction)


def square_pair(weight, direction):
    return jnp.stack([jnp.sum(weight * weight), jnp.sum(direction * direction)])


def kernel_call(kernel, grid, in_specs, out_specs, out_shape, scratch, args, aliases=None, mib=1):
    return pl.pallas_call(
        kernel,
        grid_spec=pltpu.PrefetchScalarGridSpec(
            num_scalar_prefetch=1,
            grid=grid,
            in_specs=in_specs,
            out_specs=out_specs,
            scratch_shapes=scratch,
        ),
        out_shape=out_shape,
        input_output_aliases=aliases or {},
        compiler_params=pltpu.CompilerParams(vmem_limit_bytes=48 * MIB),
        cost_estimate=pl.CostEstimate(flops=0, bytes_accessed=mib * MIB, transcendentals=0),
    )(*args)


SCALARS = pl.BlockSpec(memory_space=pltpu.SMEM)


def norm_kernel(where, grad, *refs):
    sums = refs[-1]
    groups = [refs[:3], refs[3:6]][: len(refs) // 3]
    rows = groups[0][0].shape[0]
    zero = jnp.zeros((8, groups[0][0].shape[1]), wide)
    for k, (p, m, v) in enumerate(groups):

        def body(at, total):
            here = pl.ds(pl.multiple_of(at * 32, 32), 32)
            weight = p[here, :]
            direction = lamb_moments(
                weight, grad[here, :].astype(wide), m[here, :], v[here, :], decay_rate
            )[2]
            return tuple(
                t + (sq[:8] + sq[8:16]) + (sq[16:24] + sq[24:])
                for t, sq in zip(total, (weight * weight, direction * direction))
            )

        total = lax.fori_loop(0, rows // 32, body, (zero, zero))
        mine = 1.0 if len(groups) == 1 else ((where[0] >> 1) == k).astype(wide)
        for j in range(2):
            sums[2 * k + j] = jnp.sum(total[j]) * mine


def norm_pairs_kernel(where, grad, p, m, v, sums):
    rows, cols = grad.shape
    tiles = cols // 128
    side = where[0] >> 1
    zero = jnp.zeros((8, 128), wide)
    total = [zero, zero]
    for tile in range(tiles):
        here = pl.ds(2 * tile + side, rows, stride=2 * tiles)
        weight = p[here, :]
        direction = lamb_moments(
            weight, grad[:, tile * 128 : (tile + 1) * 128].astype(wide), m[here, :], v[here, :], decay_rate
        )[2]
        for j, sq in enumerate((weight * weight, direction * direction)):
            total[j] = total[j] + jnp.sum((sq).reshape(rows // 8, 8, 128), axis=0)
    for j in range(2):
        sums[j] = jnp.sum(total[j])


def share_norms(where, grad, states, rows, pairs=False):
    specs, args = [], []
    for state, at in states:
        for array in state:
            if pairs:
                spec = pl.BlockSpec(
                    (rows, array.shape[1]), lambda i, w, at=at: (at + (w[0] & 1), 0)
                )
            elif len(states) == 2:
                spec = pl.BlockSpec(
                    (rows, array.shape[1]), lambda i, w, at=at: (at + (w[0] & 1), 0)
                )
            else:
                spec = pl.BlockSpec((rows, array.shape[1]), lambda i, w, at=at: (at + w[0], 0))
            specs.append(spec)
            args.append(array)
    return kernel_call(
        norm_pairs_kernel if pairs else norm_kernel,
        (1,),
        [whole_spec(grad.shape)] + specs,
        SCALARS,
        jax.ShapeDtypeStruct((2 * len(states),), wide),
        [],
        (where, grad, *args),
    )


def lamb_loop(refs, outs, ratio, rows, step, pick):
    p, m, v = refs

    def body(at, carry):
        here = pl.ds(pl.multiple_of(at * step, step), step)
        weight = p[here, :]
        first_new, second_new, direction = lamb_moments(
            weight, pick(here), m[here, :], v[here, :], decay_rate
        )
        outs[0][here, :] = weight - ratio * direction
        outs[1][here, :] = first_new
        outs[2][here, :] = second_new
        return carry

    lax.fori_loop(0, rows // step, body, 0)


def lamb_plain(half_of_block, where, ratio, part, got, p, m, v, *outs):
    use = half_of_block(pl.program_id(0)) == (where[0] >> 1)

    def pick(here):
        return jnp.where(use, part[here, :].astype(wide), got[here, :].astype(wide))

    lamb_loop((p, m, v), outs, ratio[0], p.shape[0], 64, pick)


def lamb_pairs(where, ratio, part, got, p, m, v, p_out, m_out, v_out, mixed):
    rows, cols = part.shape
    tiles = cols // 128
    for value, order in ((0, (part, got)), (1, (got, part))):

        @pl.when((where[0] >> 1) == value)
        def _():
            for tile in range(tiles):
                for side, ref in enumerate(order):
                    mixed[pl.ds(2 * tile + side, rows, stride=2 * tiles), :] = ref[
                        :, tile * 128 : (tile + 1) * 128
                    ].astype(wide)

    lamb_loop(
        (p, m, v), (p_out, m_out, v_out), ratio[0], p.shape[0], 192, lambda here: mixed[here, :]
    )


def lamb_call(kernel, where, ratio, grad, grad_block, grad_at, state, block, start, count, before, scratch):
    rows, cols = state[0].shape
    flat = pl.BlockSpec((block, cols), lambda i, w: (i + start, 0))
    grad_spec = pl.BlockSpec((grad_block, grad[0].shape[1]), lambda i, w: (grad_at(i), 0))
    whole = jax.ShapeDtypeStruct((rows, cols), wide)
    args = [where, ratio, *grad, *state]
    specs = [SCALARS, grad_spec, grad_spec, flat, flat, flat]
    run, aliases = kernel, {}
    if before is not None:
        aliases = {len(args) + k: k for k in range(3)}

        def run(*refs):
            kernel(*refs[: len(args)], *refs[len(args) + 3 :])

    return list(
        kernel_call(
            run,
            (count,),
            specs + [pl.BlockSpec(memory_space=pl.ANY)] * len(aliases),
            [flat, flat, flat],
            [whole, whole, whole],
            scratch,
            (*args, *(before or [])),
            aliases,
            mib=26 * count * block * cols // MIB,
        )
    )


def to_linear(values):
    rows, sides, cols = values.shape
    split = with_layout_constraint(
        values.reshape(rows, sides, cols // 128, 128), Layout(major_to_minor=(0, 2, 1, 3))
    )
    return split.transpose(0, 2, 1, 3).reshape(rows * sides * cols // 128, 128)


def from_linear(values, rows, sides):
    cols = values.size // (rows * sides)
    split = values.reshape(rows, cols // 128, sides, 128).transpose(0, 2, 1, 3)
    split = with_layout_constraint(split, Layout(major_to_minor=(0, 2, 1, 3)))
    return split.reshape(rows, sides, cols)


def apply_trust(weight, direction, norms):
    return weight - learn_rate * (norms[0] / (norms[1] + adam_eps)) * direction


def flip(values, bit):
    size = lax.axis_size("dp")
    return lax.ppermute(values, "dp", [(i, i ^ (1 << bit)) for i in range(size)])


def dp_bit(bit):
    return (lax.axis_index("dp") >> bit) & 1


def rows_of(values, start, rows):
    return lax.dynamic_slice_in_dim(values, start, rows, 0)


def total_of(pieces):
    total = pieces[0].astype(wide)
    for piece in pieces[1:]:
        total = total + piece.astype(wide)
    return total


def tie(values, *deps):
    return lax.optimization_barrier((values, *deps))[0]


def low_total(pieces):
    return total_of(pieces).astype(low)


def keep_or_join(bit, part, other):
    return jnp.where(
        dp_bit(bit) == 0,
        jnp.concatenate([part, other]),
        jnp.concatenate([other, part]),
    )


def share_of(weight, order):
    rows = weight.shape[0] // (1 << len(order))
    index = 0
    for bit in order:
        index = 2 * index + dp_bit(bit)
    return rows_of(weight, index * rows, rows)


def half_of(piece, place):
    rows = piece.shape[-2] // 2
    return lax.dynamic_slice_in_dim(piece, place * rows, rows, piece.ndim - 2)


def chunk_sum(chunk, order, keep):
    bits = {"y": 0, "l": 1}
    steps = [name if name == "x" else bits[name] for name in order]
    pieces = [chunk]
    for step in steps:
        if step == "x":
            whole = len(pieces) == 1
            got = yield step, pieces[0][1] if whole else low_total([piece[1] for piece in pieces])
            pieces = [piece[0] for piece in pieces] + [got]
        else:
            here = dp_bit(step)
            got = yield step, low_total([half_of(piece, 1 - here) for piece in pieces])
            pieces = [half_of(piece, here) for piece in pieces] + [got]
    part = low_total(pieces)
    for step in range((lax.axis_size("dp") - 1).bit_length()):
        if step not in steps:
            got = yield step, part
            part = low_total([part, got])
    keep(part)
    first, second = [step for step in steps if step != "x"]
    got = yield second, part
    part = keep_or_join(second, part, got)
    got = yield first, part
    return part, got


def norm_sum(values):
    for step in ("x", "row", 1, 0):
        got = yield step, values
        values = values + got
    return values


def where_of(order):
    bits = {"y": 0, "l": 1}
    first, second = [bits[name] for name in order if name != "x"]
    return (2 * dp_bit(first) + dp_bit(second)).astype(jnp.int32).reshape(1)


def move(step, send):
    if step == "row":
        return swap(send, "row")
    return swap(send, "col") if step == "x" else flip(send, step)


class Turns:
    def __init__(self):
        self.chunks = {}
        self.arrivals = {}
        self.seen = {}
        self.done = {}
        self.shares = {}
        self.after = ()

    def add(self, name, chunk, order):
        self.chunks[name] = chunk_sum(chunk, order, functools.partial(self.shares.__setitem__, name))

    def add_norms(self, name, values):
        self.chunks[name] = norm_sum(values)

    def turn(self, name):
        got = self.arrivals.get(name)
        try:
            if got is None:
                self.seen[name] = []
                step, send = next(self.chunks[name])
                send = tie(send, *self.after)
            else:
                got = tie(got, *self.after)
                self.seen[name].append(got)
                step, send = self.chunks[name].send(got)
        except StopIteration as end:
            self.done[name] = end.value
            return
        self.arrivals[name] = move(step, send)
        self.after = (send,)

    def run(self, names):
        for name in names:
            if name not in self.done:
                self.turn(name)

    def reach_shares(self, names):
        while any(name not in self.shares for name in names):
            self.run([name for name in names if name not in self.shares])

    def finish(self):
        while len(self.done) < len(self.chunks):
            self.run(self.chunks)


def deinterleave(pairs, gate, up):
    rows, cols = gate.shape
    tiles = cols // 128
    for tile in range(tiles):
        for side, out in enumerate((gate, up)):
            out[:, tile * 128 : (tile + 1) * 128] = pairs[
                pl.ds(2 * tile + side, rows, stride=2 * tiles), :
            ].astype(low)


def split_pairs(linear, rows, cols):
    block = 64
    half = jax.ShapeDtypeStruct((rows, cols), low)
    out_spec = pl.BlockSpec((block, cols), lambda i: (i, 0))
    return pl.pallas_call(
        deinterleave,
        grid=(rows // block,),
        in_specs=[pl.BlockSpec((block * 2 * cols // 128, 128), lambda i: (i, 0))],
        out_specs=[out_spec, out_spec],
        out_shape=[half, half],
        compiler_params=pltpu.CompilerParams(vmem_limit_bytes=24 * MIB),
        cost_estimate=pl.CostEstimate(
            flops=rows * cols, bytes_accessed=12 * rows * cols, transcendentals=0
        ),
    )(linear)


def dot_of(left, right, left_dim, right_dim):
    return lax.dot_general(
        left, right, (((left_dim,), (right_dim,)), ((), ())), preferred_element_type=wide
    )


def local_call(kernel, grid, in_specs, out_specs, out_shape, scratch, args, prefetch=0):
    return pl.pallas_call(
        kernel,
        grid_spec=pltpu.PrefetchScalarGridSpec(
            num_scalar_prefetch=prefetch,
            grid=grid,
            in_specs=in_specs,
            out_specs=out_specs,
            scratch_shapes=scratch,
        ),
        out_shape=out_shape,
        compiler_params=pltpu.CompilerParams(vmem_limit_bytes=48 * MIB),
        cost_estimate=pl.CostEstimate(flops=0, bytes_accessed=MIB, transcendentals=0),
    )(*args)


def whole_spec(shape):
    return pl.BlockSpec(shape, lambda *_: (0,) * len(shape))


def shape_of(dims, kind):
    return jax.ShapeDtypeStruct(dims, kind)


def row_scale(halves):
    total = sum(jnp.sum(half * half, axis=1, keepdims=True) for half in halves)
    return lax.rsqrt(total / D + norm_eps)


def branch_kernel(tok, gains, taps, own, other, n1, gate_b, gate_c, gate_x, conv, hidden, part0, part1, ext):
    long, width = n1.shape[1:]
    rows = conv.shape[0]
    step = long // 3

    def gates(at, carry):
        here = pl.ds(pl.multiple_of(at * step, step), step)
        halves = [tok[h, here, :].astype(wide) for h in range(2)]
        scale = row_scale(halves)
        for h in range(2):
            n1[h, here, :] = (halves[h] * scale * gains[h]).astype(low)
        for g, out in enumerate((gate_b, gate_c, gate_x)):
            w = slice(g * width, (g + 1) * width)
            out[here, :] = dot_of(n1[0, here, :], own[w, :], 1, 0) + dot_of(
                n1[1, here, :], other[w, :], 1, 0
            )
        return carry

    lax.fori_loop(0, 3, gates, 0)
    ext[8 : 8 + rows, :] = gate_b[:rows, :] * gate_x[:rows, :]
    ext[6:8, :] = gate_b[rows : rows + 2, :] * gate_x[rows : rows + 2, :]
    w_out = slice(3 * width, 4 * width)
    quarter = rows // 4
    for at in range(4):
        start = at * quarter
        taken = slice(start, start + quarter)
        value = sum(taps[k] * ext[start + 6 + k : start + 6 + k + quarter, :] for k in range(3))
        conv[taken, :] = value
        low_hidden = (gate_c[taken, :] * value).astype(low)
        hidden[taken, :] = low_hidden
        for part, weight in ((part0, own), (part1, other)):
            part[taken, :] = dot_of(low_hidden, weight[w_out, :], 1, 0).astype(low)


def branch_forward(tok, rows, tails, gains, taps, own, other):
    width = tok.shape[2]
    gate = shape_of((rows + tails, width), wide)
    outs = [
        shape_of((2, rows + tails, width), low),
        gate,
        gate,
        gate,
        shape_of((rows, width), wide),
        shape_of((rows, width), low),
        shape_of((rows, width), low),
        shape_of((rows, width), low),
    ]
    args = (tok, gains, taps, own, other)
    return local_call(
        branch_kernel,
        (1,),
        [whole_spec(a.shape) for a in args],
        [whole_spec(o.shape) for o in outs],
        outs,
        [pltpu.VMEM((rows + 8, width), wide)],
        args,
    )


def piece_at(bits, which, piece, width):
    place = bits[which] if piece == 0 else 1 - bits[which]
    return pl.ds(pl.multiple_of(place * width, width), width)


def ffn_kernel(bits, tok, mine0, mine1, theirs0, theirs1, gains, g0, g1, g2, u0, u1, u2, n2, res, gate, up, act):
    width = g1.shape[0]

    @pl.when(pl.program_id(0) == 0)
    def _():
        for h, (mine, theirs) in enumerate(((mine0, theirs0), (mine1, theirs1))):
            res[h] = tok[h, : res.shape[1], :].astype(wide) + (
                mine[...].astype(wide) + theirs[...].astype(wide)
            )
        scale = row_scale([res[0], res[1]])
        for h in range(2):
            n2[h] = (res[h] * scale * gains[h]).astype(low)

    for which, (out, w0, w1, w2) in enumerate(((gate, g0, g1, g2), (up, u0, u1, u2))):
        total = dot_of(n2[0], w0[...], 1, 0)
        for piece, w in enumerate((w1, w2)):
            total += dot_of(n2[1, :, piece_at(bits, which, piece, width)], w[...], 1, 0)
        out[...] = total
    value = gate[...]
    act[...] = (value * jax.nn.sigmoid(value) * up[...]).astype(low)


def ffn_forward(bits, tok, mine, theirs, gains, weights):
    rows, width = mine[0].shape
    cols = weights[0].shape[1]
    tile = cols // 3
    both = (2, rows, width)
    full = whole_spec(both)
    wide_tile = pl.BlockSpec((rows, tile), lambda i, *_: (0, i))
    weight_specs = [pl.BlockSpec((w.shape[0], tile), lambda i, *_: (0, i)) for w in weights]
    return local_call(
        ffn_kernel,
        (3,),
        [whole_spec(tok.shape)]
        + [whole_spec((rows, width))] * 4
        + [whole_spec(gains.shape)]
        + weight_specs,
        [full, full, wide_tile, wide_tile, wide_tile],
        [
            shape_of(both, low),
            shape_of(both, wide),
            shape_of((rows, cols), wide),
            shape_of((rows, cols), wide),
            shape_of((rows, cols), low),
        ],
        [],
        (bits, tok, *mine, *theirs, gains, *weights),
        prefetch=1,
    )


def ffn_back_kernel(
    bits, cot, d_own, d_other, gate, up, g0, g1, g2, u0, u1, u2, g_gate, g_up, part0, part1, total
):
    width = g1.shape[0]

    @pl.when(pl.program_id(0) == 0)
    def _():
        total[...] = jnp.zeros_like(total)

    start = cot.shape[1] - gate.shape[0]
    g_act = dot_of(cot[0, start:, :], d_own[...], 1, 1) + dot_of(cot[1, start:, :], d_other[...], 1, 1)
    value = gate[...]
    sigma = jax.nn.sigmoid(value)
    g_gate[...] = (g_act * up[...] * sigma * (1.0 + value * (1.0 - sigma))).astype(low)
    g_up[...] = (g_act * (value * sigma)).astype(low)
    total[0] += dot_of(g_gate[...], g0[...], 1, 1) + dot_of(g_up[...], u0[...], 1, 1)
    for which, (grad, w1, w2) in enumerate(((g_gate, g1, g2), (g_up, u1, u2))):
        for piece, w in enumerate((w1, w2)):
            total[1, :, piece_at(bits, which, piece, width)] += dot_of(grad[...], w[...], 1, 1)

    @pl.when(pl.program_id(0) == pl.num_programs(0) - 1)
    def _():
        part0[...] = total[0].astype(low)
        part1[...] = total[1].astype(low)


def ffn_backward(bits, cot, downs, gate, up, weights):
    rows, cols = gate.shape
    tile = cols // 3
    part = (rows, cot.shape[2])
    wide_tile = pl.BlockSpec((rows, tile), lambda i, *_: (0, i))
    weight_specs = [pl.BlockSpec((w.shape[0], tile), lambda i, *_: (0, i)) for w in weights]
    down_spec = pl.BlockSpec((tile, downs[0].shape[1]), lambda i, *_: (i, 0))
    return local_call(
        ffn_back_kernel,
        (3,),
        [whole_spec(cot.shape), down_spec, down_spec, wide_tile, wide_tile] + weight_specs,
        [wide_tile, wide_tile, whole_spec(part), whole_spec(part)],
        [shape_of((rows, cols), low)] * 2 + [shape_of(part, low)] * 2,
        [pltpu.VMEM((2, *part), wide)],
        (bits, cot, *downs, gate, up, *weights),
        prefetch=1,
    )


def put(outs, half, rows, value):
    if len(outs) == 2:
        outs[half][rows, :] = value.astype(low)
    else:
        outs[0][half, rows, :] = value.astype(low)


def chunk_outs(split, rows, cols):
    if split:
        return [whole_spec((rows, cols))] * 2, [shape_of((rows, cols), low)] * 2
    return [whole_spec((2, rows, cols))], [shape_of((2, rows, cols), low)]


def pair_grad_kernel(items, n2, g_gate, g_up, *outs):
    rows = outs[0].shape[-2] // 2
    for at, split in items:
        count = 2 if split else 1
        mine, outs = outs[:count], outs[count:]
        for h in range(2):
            left = n2[h, :, at * rows : (at + 1) * rows]
            for side, grad in enumerate((g_gate, g_up)):
                put(mine, h, slice(side * rows, (side + 1) * rows), dot_of(left, grad[...], 0, 0))


def pair_grads(n2, g_gate, g_up, items, rows):
    specs, shapes = [], []
    for _, split in items:
        more = chunk_outs(split, 2 * rows, g_gate.shape[1])
        specs += more[0]
        shapes += more[1]
    outs = local_call(
        functools.partial(pair_grad_kernel, items),
        (1,),
        [whole_spec(n2.shape), whole_spec(g_gate.shape), whole_spec(g_up.shape)],
        specs,
        shapes,
        [],
        (n2, g_gate, g_up),
    )
    found = []
    for _, split in items:
        count = 2 if split else 1
        found.append(tuple(outs[:count]) if split else outs[0])
        outs = outs[count:]
    return found


def down_grad_kernel(act, cot, *outs):
    start = cot.shape[1] - act.shape[0]
    for h in range(2):
        put(outs, h, slice(None), dot_of(act[...], cot[h, start:, :], 0, 0))


def down_grads(act, cot, at, rows, split):
    specs, shapes = chunk_outs(split, rows, cot.shape[2])
    outs = local_call(
        down_grad_kernel,
        (1,),
        [pl.BlockSpec((act.shape[0], rows), lambda i: (0, at)), whole_spec(cot.shape)],
        specs,
        shapes,
        [],
        (act, cot),
    )
    return tuple(outs) if split else outs[0]


def branch_back_kernel(
    mine0, mine1, theirs0, theirs1, res, cot, gains, taps, own, other, gate_b, gate_c, gate_x, conv,
    g_res, g_low, g_proj, gain_grad, tap_grad, ext, ext_grad,
):
    _, rows, width = res.shape
    scale = row_scale([res[0], res[1]])
    grads = [
        mine[...].astype(wide) + theirs[...].astype(wide)
        for mine, theirs in ((mine0, theirs0), (mine1, theirs1))
    ]
    inner = sum(
        jnp.sum(grads[h] * gains[h] * res[h], axis=1, keepdims=True) for h in range(2)
    )
    factor = scale * scale * scale * inner / D
    for h in range(2):
        gain_grad[h] = jnp.sum(grads[h] * res[h] * scale, axis=0, keepdims=True)
        value = cot[h, cot.shape[1] - rows :, :].astype(wide) + (scale * (grads[h] * gains[h]) - res[h] * factor)
        g_res[h] = value
        g_low[h] = value.astype(low)
    g_hidden = dot_of(g_low[0], own[...], 1, 1) + dot_of(g_low[1], other[...], 1, 1)
    g_proj[1, :rows, :] = (g_hidden * conv[...]).astype(low)
    g_conv = g_hidden * gate_c[:rows, :]
    ext_grad[:rows, :] = g_conv
    ext_grad[rows:, :] = jnp.zeros((8, width), wide)
    ext[8 : 8 + rows, :] = gate_b[:rows, :] * gate_x[:rows, :]
    ext[6:8, :] = gate_b[rows : rows + 2, :] * gate_x[rows : rows + 2, :]
    for k in range(3):
        tap_grad[k : k + 1, :] = jnp.sum(
            g_conv * ext[6 + k : 6 + k + rows, :], axis=0, keepdims=True
        )
    g_mixed = sum(taps[2 - k] * ext_grad[k : k + rows, :] for k in range(3))
    g_proj[0, :rows, :] = (g_mixed * gate_x[:rows, :]).astype(low)
    g_proj[2, :rows, :] = (g_mixed * gate_b[:rows, :]).astype(low)
    tails = g_proj.shape[1] - rows
    row = lax.broadcasted_iota(jnp.int32, (tails, width), 0)
    first, second = ext_grad[0:1, :], ext_grad[1:2, :]
    g_before = jnp.where(
        row == 0,
        taps[0] * first,
        jnp.where(row == 1, taps[1] * first + taps[0] * second, 0.0),
    )
    g_proj[0, rows:, :] = (g_before * gate_x[rows:, :]).astype(low)
    g_proj[1, rows:, :] = jnp.zeros((tails, width), low)
    g_proj[2, rows:, :] = (g_before * gate_b[rows:, :]).astype(low)


def branch_backward(mine, theirs, res, cot, gains, taps, own, other, gates, conv):
    _, rows, width = res.shape
    long = gates[0].shape[0]
    out_weight = pl.BlockSpec((width, width), lambda i, *_: (3, 0))
    outs = [
        shape_of(res.shape, wide),
        shape_of(res.shape, low),
        shape_of((3, long, width), low),
        shape_of((2, 1, width), wide),
        shape_of((3, width), wide),
    ]
    full = whole_spec(res.shape)
    return local_call(
        branch_back_kernel,
        (1,),
        [whole_spec((rows, width))] * 4
        + [full, whole_spec(cot.shape), whole_spec(gains.shape), whole_spec(taps.shape)]
        + [out_weight, out_weight]
        + [whole_spec(g.shape) for g in gates]
        + [whole_spec(conv.shape)],
        [whole_spec(o.shape) for o in outs],
        outs,
        [pltpu.VMEM((rows + 8, width), wide), pltpu.VMEM((rows + 8, width), wide)],
        (*mine, *theirs, res, cot, gains, taps, own, other, *gates, conv),
    )


def branch_grad_kernel(left0, left1, right0, right1, own, other):
    rows = own.shape[0] // 2
    for h, out in enumerate((own, other)):
        for k, (left, right) in enumerate(((left0, right0), (left1, right1))):
            one = left[h] if len(left.shape) == 3 else left[...]
            two = right[h] if k == 1 and len(left.shape) == 2 else right[0]
            out[k * rows : (k + 1) * rows, :] = dot_of(one, two, 0, 0).astype(low)


def branch_grads(n1, g_proj, gate, second):
    width = n1.shape[2]
    gate_spec = pl.BlockSpec((1, *g_proj.shape[1:]), lambda i: (gate, 0, 0))
    if second is None:
        left, right = n1, g_proj
        right_spec = pl.BlockSpec((1, *g_proj.shape[1:]), lambda i: (gate + 1, 0, 0))
    else:
        left, right = second
        right_spec = whole_spec(right.shape)
    specs, shapes = chunk_outs(True, 2 * width, width)
    return local_call(
        branch_grad_kernel,
        (1,),
        [whole_spec(n1.shape), whole_spec(left.shape), gate_spec, right_spec],
        specs,
        shapes,
        [],
        (n1, left, g_proj, right),
    )


def shards(
    tokens,
    cotangent,
    input_projection_weight,
    conv_weight,
    output_projection_weight,
    norm_gains,
    gate_up_weight,
    down_projection_weight,
    in_first,
    in_second,
    conv_first,
    conv_second,
    out_first,
    out_second,
    gain_first,
    gain_second,
    gu_first,
    gu_second,
    down_first,
    down_second,
):
    feat_cols = tokens.shape[1]
    branch_cols = conv_weight.shape[1]
    hidden_cols = down_projection_weight.shape[0]
    block_rows = tokens.shape[0]
    seq_len = max(SEQ_LEAST, block_rows * lax.axis_size("dp") * lax.axis_size("col"))
    data_pos = lax.axis_index("dp")
    row_pos = lax.axis_index("row")
    col_pos = lax.axis_index("col")
    home = row_pos == col_pos
    tail_rows = 16

    in_low = jnp.transpose(input_projection_weight, (1, 0, 2)).astype(low).reshape(-1, branch_cols)
    io_low = jnp.concatenate([in_low, output_projection_weight.astype(low)])
    io_share = share_of(io_low, (1, 0))
    io_got = swap(io_share, "col")
    row_start = (data_pos * lax.axis_size("row") + row_pos) * block_rows
    tail = from_behind(tokens[-2:], ("dp", "row"), 1)
    tail = jnp.where(row_start % seq_len != 0, tail, jnp.zeros_like(tail))
    spare = jnp.zeros((tail_rows - 8, feat_cols), low)
    gain_parts = []
    left = norm_gains
    for _ in range(3):
        gain_parts.append(lax.reduce_precision(left, 8, 7))
        left = left - gain_parts[-1]
    gain_parts = jnp.concatenate(gain_parts).astype(low)
    extra = tie(jnp.concatenate([tail, gain_parts, spare]))
    block = jnp.concatenate([tie(tokens, io_got), extra, cotangent])
    away = to_home(block)
    gu_weight = to_linear(gate_up_weight)
    gate_low, up_low = split_pairs(gu_weight, feat_cols, hidden_cols)
    down_low = down_projection_weight.astype(low)
    both = jnp.stack([block, away])
    both = jnp.where(home, both, home_to_sibling(both))
    gains = both[:, block_rows + 2 : block_rows + 8].astype(wide)
    gains = gains[:, 0:2] + gains[:, 2:4] + gains[:, 4:6]
    gains = [gains[:, k : k + 1] for k in range(2)]
    gate_got = swap(tie(share_of(gate_low, (1, 0)), io_got), "col")
    up_got = swap(tie(share_of(up_low, (0, 1)), gate_got), "col")
    down_got = swap(tie(down_low, up_got), "col")
    io_pair = keep_or_join(0, io_got, flip(io_got, 0))
    io_other = keep_or_join(1, io_pair, flip(io_pair, 1))
    gate_pair = keep_or_join(0, gate_got, flip(tie(gate_got, io_pair), 0))
    up_pair = keep_or_join(1, up_got, flip(tie(up_got, io_pair), 1))
    gate_more = flip(gate_pair, 1)
    up_more = flip(up_pair, 0)
    weights = [gate_low, gate_pair, gate_more, up_low, up_pair, up_more]
    bits = jnp.stack([dp_bit(1), dp_bit(0)]).astype(jnp.int32)
    downs = [down_low, down_got]

    n1, gate_b, gate_c, gate_x, conv, hidden, *branch = branch_forward(
        both, block_rows, tail_rows, gains[0], conv_weight, io_low, io_other
    )
    n2, res, gate, upper, act = ffn_forward(
        bits, both, branch, swap_halves(branch), gains[1], weights
    )

    turns = Turns()
    orders = dict(D="xyl", d="ylx", a="xyl", b="lyx", c="xyl", e="lyx", I="xyl", i="xyl")
    down_half = hidden_cols // 2
    for k, name in enumerate("Dd"):
        split = orders[name][0] == "x"
        turns.add(name, down_grads(act, both, k, down_half, split), orders[name])
    turns.run("Dd")
    g_gate, g_up, *part_two = ffn_backward(
        bits, tie(both, *turns.after), downs, gate, upper, weights
    )
    quarter = feat_cols // 4
    for names in ("ab", "ce"):
        items = [("abce".index(name), orders[name][0] == "x") for name in names]
        for name, chunk in zip(names, pair_grads(n2, g_gate, g_up, items, quarter)):
            turns.add(name, chunk, orders[name])
    turns.run("abcDe")
    g_res, g_branch, g_proj, gain_two_grad, conv_grad = branch_backward(
        part_two,
        swap_halves(part_two),
        tie(res, *turns.after),
        both,
        gains[1],
        conv_weight,
        io_low,
        io_other,
        (gate_b, gate_c, gate_x),
        conv,
    )
    turns.add("I", branch_grads(n1, g_proj, 0, None), orders["I"])
    io_last = branch_grads(n1, g_proj, 2, (hidden, g_branch))
    turns.after += tuple(io_last)
    turns.run("IdabD")

    g_late = tie(g_proj, *turns.after)
    io_half = [half.reshape(4, feat_cols, branch_cols) for half in (io_low, io_other)]
    g_part = jnp.stack(
        [sum(mul_t(g_late[g], io_half[h][g]) for g in range(3)).astype(low) for h in range(2)]
    )
    g_long = g_part.astype(wide) + swap(g_part, "row").astype(wide)
    tok = both[:, : block_rows + 2].astype(wide)
    scale = lax.rsqrt(jnp.sum(tok * tok, axis=(0, 2)) / D + norm_eps)[None, :, None]
    gain_one_grad = jnp.sum(g_long[:, : block_rows + 2] * tok * scale, axis=1)
    small = [
        jnp.concatenate([conv_grad, gain_one_grad[h : h + 1], gain_two_grad[h]]) for h in range(2)
    ]
    spare = jnp.zeros((16, feat_cols), low)
    small = [jnp.pad(part, ((0, 11), (0, 0))).astype(low) for part in small]
    io_long = []
    for h in range(2):
        pieces = jnp.split(io_last[h], 4)
        io_long.append(
            jnp.concatenate(
                [pieces[0], small[h], pieces[1], spare, pieces[2], spare, pieces[3], spare]
            )
        )
    turns.add("i", io_long, orders["i"])
    turns.run("eiacbdDIcaeDciIabDdcieIDabd")

    def in_flat(values):
        return jnp.transpose(values, (1, 0, 2)).reshape(3 * feat_cols, branch_cols)

    def in_back(values):
        return jnp.transpose(values.reshape(3, feat_cols, branch_cols), (1, 0, 2))

    wheres = {name: where_of(orders[name]) for name in orders}
    down_state = (down_projection_weight, down_first, down_second)
    gu_state = (gu_weight, to_linear(gu_first), to_linear(gu_second))
    in_state = (in_flat(input_projection_weight), in_flat(in_first), in_flat(in_second))
    out_state = (output_projection_weight, out_first, out_second)
    pairs = 2 * hidden_cols // 128

    shares = turns.shares
    part_rows = feat_cols // 2
    turns.reach_shares("Dd")
    down_squares = sum(
        share_norms(wheres[n], shares[n], [(down_state, 4 * k)], down_half // 4)
        for k, n in enumerate("Dd")
    )
    turns.add_norms("p", down_squares)
    turns.run("pacpibpcep")
    turns.reach_shares("abce")
    gu_squares = sum(
        share_norms(wheres[n], shares[n], [(gu_state, 2 * k)], quarter // 2 * pairs, pairs=True)
        for k, n in enumerate("abce")
    )
    turns.add_norms("n", gu_squares)
    turns.run("nIdnbipn")
    turns.reach_shares("Ii")
    io_squares = share_norms(wheres["i"], shares["i"], [(in_state, 4), (out_state, 0)], part_rows)
    in_squares = share_norms(wheres["I"], shares["I"], [(in_state, 0)], part_rows)
    turns.add_norms("m", io_squares + jnp.pad(in_squares, (0, 2)))
    turns.run("mednIenimIimmm")
    turns.finish()
    sums, seen = turns.done, turns.seen

    back = tie(g_long[::-1, block_rows : block_rows + 2], seen["i"][4])
    back = from_behind(back, ("dp", "col"), -1)
    g_n1 = g_long[:, :block_rows].at[:, -2:].add(back)
    tok, scale = tok[:, :block_rows], scale[:, :block_rows]
    weighted = g_n1 * gains[0]
    inner = jnp.sum(weighted * tok, axis=(0, 2))[None, :, None]
    tok_half = (g_res + (scale * weighted - tok * (scale * scale * scale * inner / D))).astype(low)
    token_grad = jnp.where(home, tok_half[0], home_to_away(tok_half[1]))
    act = tie(act, seen["D"][1])
    ffn = jnp.stack([mul(act, downs[h]) for h in range(2)])
    out_half = (res + (ffn + sibling_to_home(ffn.astype(low)).astype(wide))).astype(low)
    output = jnp.where(home, out_half[0], home_to_away(out_half[1]))

    def gu_back(values):
        return from_linear(values, feat_cols, 2)

    def ratio_of(norms):
        norms = jnp.sqrt(norms)
        return norms, (learn_rate * (norms[0] / (norms[1] + adam_eps))).reshape(1)

    (gu_norms, gu_ratio), (down_norms, down_ratio) = [ratio_of(sums[name]) for name in "np"]
    (in_norms, in_ratio), (out_norms, out_ratio) = [ratio_of(sums["m"][k : k + 2]) for k in (0, 2)]

    def later_half(count):
        return functools.partial(lamb_plain, lambda i: (i >= count // 2).astype(jnp.int32))

    def fixed_half(half):
        return functools.partial(lamb_plain, lambda i: half)

    last = sums["i"]
    small = [part[part_rows : part_rows + 5] for part in last]
    small = jnp.where((wheres["i"][0] >> 1) == 0, small[0], small[1]).astype(wide)
    conv_grad, gains_grad = small[:3], small[3:]
    conv_m, conv_v, conv_u = lamb_moments(conv_weight, conv_grad, conv_first, conv_second, 0.0)
    gain_m, gain_v, gain_u = lamb_moments(norm_gains, gains_grad, gain_first, gain_second, 0.0)
    col_first = (col_pos == 0).astype(wide)
    row_first = (row_pos == 0).astype(wide)
    small_weight = jnp.concatenate([conv_weight, norm_gains])
    small_direction = jnp.concatenate([conv_u, gain_u])
    squares = jnp.stack(
        [
            jnp.sum(small_weight * small_weight, axis=1),
            jnp.sum(small_direction * small_direction, axis=1),
        ],
        axis=1,
    )
    small_norms = jnp.concatenate(
        [jnp.sum(squares[:3], axis=0, keepdims=True) * col_first, squares[3:] * row_first]
    )
    down_sums = [sums[name] for name in "Dd"]
    pair_sums = [sums[name] for name in "abce"]
    row_norms = small_norms + swap(small_norms, "row")
    pair_sums[2] = [tie(part, last[1]) for part in pair_sums[2]]
    pair_sums[1] = [tie(part, small_norms) for part in pair_sums[1]]
    pair_sums[3] = [tie(part, row_norms) for part in pair_sums[3]]
    down_sums[1] = [tie(part, row_norms) for part in down_sums[1]]
    down_new = None
    for k in (0, 1):
        name = "Dd"[k]
        block = down_half // 6
        down_new = lamb_call(
            later_half(6), wheres[name], down_ratio, down_sums[k], block, lambda i: i % 3,
            down_state, block, 6 * k, 6, down_new, [],
        )
    gu_new = None
    gu_rows = 32
    for k in (0, 2, 1, 3):
        name = "abce"[k]
        blocks = quarter // gu_rows
        gu_new = lamb_call(
            lamb_pairs, wheres[name], gu_ratio, pair_sums[k], gu_rows, lambda i: i,
            gu_state, gu_rows * pairs, k * blocks, blocks, gu_new,
            [pltpu.VMEM((gu_rows * pairs, 128), wide)],
        )
    small_norms = jnp.sqrt(row_norms + swap(row_norms, "col"))
    last = [tie(part, small_norms) for part in last]
    first_io = [tie(part, small_norms) for part in sums["I"]]
    in_new = lamb_call(
        later_half(4), wheres["I"], in_ratio, first_io, part_rows, lambda i: i % 2,
        in_state, part_rows, 0, 4, None, [],
    )
    in_new = lamb_call(
        fixed_half(0), wheres["i"], in_ratio, last, part_rows + 16, lambda i: i,
        in_state, part_rows, 4, 2, in_new, [],
    )
    out_new = lamb_call(
        fixed_half(1), wheres["i"], out_ratio, last, part_rows + 16, lambda i: i,
        out_state, part_rows, 0, 2, None, [],
    )

    trust_norms = jnp.stack(
        [
            in_norms,
            small_norms[0],
            out_norms,
            small_norms[1],
            small_norms[2],
            gu_norms,
            down_norms,
        ]
    )
    gains_new = jnp.stack(
        [
            apply_trust(norm_gains[0], gain_u[0], small_norms[1]),
            apply_trust(norm_gains[1], gain_u[1], small_norms[2]),
        ]
    )
    return (
        output,
        token_grad,
        *[in_back(values) for values in in_new],
        apply_trust(conv_weight, conv_u, small_norms[0]),
        conv_m,
        conv_v,
        *out_new,
        gains_new,
        gain_m,
        gain_v,
        *[gu_back(values) for values in gu_new],
        *down_new,
        trust_norms,
    )


def solution(mesh):
    in_specs = (
        P(("dp", "row"), "col"),
        P(("dp", "row"), "col"),
        P("col", None, "row"),
        P(None, "row"),
        P("row", "col"),
        P(None, "col"),
        P("col", None, "row"),
        P("row", "col"),
        P("col", None, "row"),
        P("col", None, "row"),
        P(None, "row"),
        P(None, "row"),
        P("row", "col"),
        P("row", "col"),
        P(None, "col"),
        P(None, "col"),
        P("col", None, "row"),
        P("col", None, "row"),
        P("row", "col"),
        P("row", "col"),
    )
    out_specs = (
        P(("dp", "row"), "col"),
        P(("dp", "row"), "col"),
        P("col", None, "row"),
        P("col", None, "row"),
        P("col", None, "row"),
        P(None, "row"),
        P(None, "row"),
        P(None, "row"),
        P("row", "col"),
        P("row", "col"),
        P("row", "col"),
        P(None, "col"),
        P(None, "col"),
        P(None, "col"),
        P("col", None, "row"),
        P("col", None, "row"),
        P("col", None, "row"),
        P("row", "col"),
        P("row", "col"),
        P("row", "col"),
        P(),
    )
    return jax.shard_map(shards, mesh=mesh, in_specs=in_specs, out_specs=out_specs, check_vma=False)
```

profile of v0, /device:TPU:0, one launch (start us, length us, event | category | flops | bytes accessed | tf_op | source)
XLA Modules:
  0.0 524.5 jit_solution(13571799617973101387)
XLA Ops:
  10.1 9.0 %collective-permute-done = bf16[512,512]{1,0:T(8,128)(2,1)} collective-permute-done((bf16[512,512]{1,0:T(8,128)(2,1)S(1)}, bf16[512,512]{1,0:T(8,128)(2,1)}, u32[]{:S(2)}, u32[]{:S(2)}) %collective-permute-start) | collective-permute-done | bytes 524320 | tf_op jit(solution)/shard_map/ppermute | solution.py:34
  33.7 8.8 %collective-permute-done.2 = bf16[1040,512]{1,0:T(8,128)(2,1)} collective-permute-done((bf16[1040,512]{1,0:T(8,128)(2,1)}, bf16[1040,512]{1,0:T(8,128)(2,1)}, u32[]{:S(2)}, u32[]{:S(2)}) %collective-permute-start.2) | collective-permute-done | bytes 1064992 | tf_op jit(solution)/shard_map/ppermute | solution.py:42
  55.4 4.2 convert_element_type.453.d_own
  61.0 5.8 %collective-permute-done.11 = bf16[128,2304]{1,0:T(8,128)(2,1)S(1)} collective-permute-done((bf16[128,2304]{1,0:T(8,128)(2,1)S(1)}, bf16[128,2304]{1,0:T(8,128)(2,1)S(1)}, u32[]{:S(2)}, u32[]{:S(2)}) %collective-permute-start.11) | collective-permute-done | bytes 589856 | tf_op jit(solution)/shard_map/ppermute | solution.py:34
  74.0 4.3 maximum_select_fusion.other
  78.3 8.2 %collective-permute-done.12 = bf16[128,2304]{1,0:T(8,128)(2,1)S(1)} collective-permute-done((bf16[128,2304]{1,0:T(8,128)(2,1)S(1)}, bf16[128,2304]{1,0:T(8,128)(2,1)S(1)}, u32[]{:S(2)}, u32[]{:S(2)}) %collective-permute-start.12) | collective-permute-done | bytes 589856 | tf_op jit(solution)/shard_map/ppermute | solution.py:271
  90.4 7.6 %shard_map.355 = (bf16[2,528,512]{2,1,0:T(8,128)(2,1)S(1)}, f32[528,512]{1,0:T(8,128)S(1)}, f32[528,512]{1,0:T(8,128)S(1)}, f32[528,512]{1,0:T(8,128)}, f32[512,...) custom-call(bf16[2,1040,512]{2,1,0:T(8,128)(2,1)} %copy-done.1, ...), custom_call_target="tpu_custom_call" | custom-call | bytes 1048576 | tf_op jit(solution)/shard_map/pallas_call | solution.py:443
  103.4 5.4 %collective-permute-done.10.g2 = bf16[256,2304]{1,0:T(8,128)(2,1)S(1)} collective-permute-done((bf16[256,2304]{1,0:T(8,128)(2,1)S(1)}, bf16[256,2304]{1,0:T(8,128)(2,1)S(1)}, u32[]{:S(2)}, u32[]{:S(2)}) %collective-permute-start.10) | collective-permute-done | bytes 1179680 | tf_op jit(solution)/shard_map/ppermute | solution.py:271
  111.0 13.6 %shard_map.357 = (bf16[2,512,512]{2,1,0:T(8,128)(2,1)S(1)}, f32[2,512,512]{2,1,0:T(8,128)}, f32[512,2304]{1,0:T(8,128)}, f32[512,2304]{1,0:T(8,128)}, bf16[512,2304]{1,0:T(8,128)(2,1)}) custom-call(s32[2]{0:T(128)S(1)} %pad_add_fusion.bits, bf16[2,1040,512]{2,1,0:T(8,128)(2,1)} %copy-done.1, bf16[512,512]{1,0:T(8,128)(2,1)S(1)} %get-tuple-element.190.mine0, ...), custom_call_target="tpu_custom_call" | custom-call | bytes 1048576 | tf_op jit(solution)/shard_map/pallas_call | solution.py:443
  140.3 16.1 %shard_map.360 = (bf16[512,2304]{1,0:T(8,128)(2,1)}, bf16[512,2304]{1,0:T(8,128)(2,1)}, bf16[512,512]{1,0:T(8,128)(2,1)S(1)}, bf16[512,512]{1,0:T(8,128)(2,1)S(1)}) custom-call(s32[2]{0:T(128)S(1)} %pad_add_fusion.bits, bf16[2,1040,512]{2,1,0:T(8,128)(2,1)} %copy-done.1, bf16[2304,512]{1,0:T(8,128)(2,1)} %convert_element_type.453.d_own, ...), custom_call_target="tpu_custom_call" | custom-call | bytes 1048576 | tf_op jit(solution)/shard_map/pallas_call | solution.py:443
  158.0 5.0 shard_map.361
  163.0 5.5 %shard_map.362 = (bf16[256,2304]{1,0:T(8,128)(2,1)S(1)}, bf16[256,2304]{1,0:T(8,128)(2,1)}, bf16[2,256,2304]{2,1,0:T(8,128)(2,1)S(1)}) custom-call(bf16[2,512,512]{2,1,0:T(8,128)(2,1)S(1)} %copy-done.28, bf16[512,2304]{1,0:T(8,128)(2,1)} %get-tuple-element.208.g_gate, bf16[512,2304]{1,0:T(8,128)(2,1)} %get-tuple-element.209.g_up), custom_call_target="tpu_custom_call" | custom-call | bytes 1048576 | tf_op jit(solution)/shard_map/pallas_call | solution.py:443
  180.9 7.2 %shard_map.363 = (f32[2,512,512]{2,1,0:T(8,128)}, bf16[2,512,512]{2,1,0:T(8,128)(2,1)S(1)}, bf16[3,528,512]{2,1,0:T(8,128)(2,1)}, f32[2,1,512]{2,1,0:T(1,128)S(1)}, f32[3,512]{1,0:T(4,128)S(1)}) custom-call(bf16[512,512]{1,0:T(8,128)(2,1)S(1)} %copy-done.53, bf16[512,512]{1,0:T(8,128)(2,1)S(1)} %copy-done.55, ...), custom_call_target="tpu_custom_call" | custom-call | bytes 1048576 | tf_op jit(solution)/shard_map/pallas_call | solution.py:443
  217.3 7.7 %collective-permute-done.25 = bf16[2,128,2304]{2,1,0:T(8,128)(2,1)S(1)} collective-permute-done((bf16[2,128,2304]{2,1,0:T(8,128)(2,1)}, bf16[2,128,2304]{2,1,0:T(8,128)(2,1)S(1)}, u32[]{:S(2)}, u32[]{:S(2)}) %collective-permute-start.25) | collective-permute-done | bytes 1179680 | tf_op jit(solution)/shard_map/ppermute | solution.py:271
  264.6 6.0 %collective-permute-done.29 = bf16[128,2304]{1,0:T(8,128)(2,1)} collective-permute-done((bf16[128,2304]{1,0:T(8,128)(2,1)}, bf16[128,2304]{1,0:T(8,128)(2,1)}, u32[]{:S(2)}, u32[]{:S(2)}) %collective-permute-start.29) | collective-permute-done | bytes 589856 | tf_op jit(solution)/shard_map/ppermute | solution.py:271
  272.3 5.0 collective-permute-done.37
  296.9 4.8 collective-permute-done.43
  311.1 10.0 %collective-permute-done.39 = bf16[64,2304]{1,0:T(8,128)(2,1)} collective-permute-done((bf16[64,2304]{1,0:T(8,128)(2,1)S(1)}, bf16[64,2304]{1,0:T(8,128)(2,1)}, u32[]{:S(2)}, u32[]{:S(2)}) %collective-permute-start.39) | collective-permute-done | bytes 294944 | tf_op jit(solution)/shard_map/ppermute | solution.py:271
  325.4 5.0 collective-permute-start.49
  333.5 9.6 %collective-permute-done.49 = bf16[256,512]{1,0:T(8,128)(2,1)S(1)} collective-permute-done((bf16[256,512]{1,0:T(8,128)(2,1)S(1)}, bf16[256,512]{1,0:T(8,128)(2,1)S(1)}, u32[]{:S(2)}, u32[]{:S(2)}) %collective-permute-start.49) | collective-permute-done | bytes 262176 | tf_op jit(solution)/shard_map/ppermute | solution.py:271
  353.2 5.6 %collective-permute-done.52 = bf16[64,2304]{1,0:T(8,128)(2,1)S(1)} collective-permute-done((bf16[64,2304]{1,0:T(8,128)(2,1)S(1)}, bf16[64,2304]{1,0:T(8,128)(2,1)S(1)}, u32[]{:S(2)}, u32[]{:S(2)}) %collective-permute-start.52) | collective-permute-done | bytes 294944 | tf_op jit(solution)/shard_map/ppermute | solution.py:271
  387.2 4.8 collective-permute-done.53
  403.7 7.7 %shard_map.381 = (f32[2304,512]{1,0:T(8,128)}, f32[2304,512]{1,0:T(8,128)}, f32[2304,512]{1,0:T(8,128)}) custom-call(s32[1]{0:T(128)} %bitcast.29.where.refs_0_, f32[1]{0:T(128)S(6)} %mul.441.ratio.refs_1_, bf16[576,512]{1,0:T(8,128)(2,1)S(1)} %copy-done.30, bf16[576,512]{1,0:T(8,128)(2,1)S(1)} %copy-done.49, f32[2304,512]{1,0:T(8,128)S(1)} %copy-done.5, ...), custom_call_target="tpu_custom_call" | custom-call | bytes 14680064 | tf_op jit(solution)/shard_map/pallas_call | solution.py:89
  423.6 6.5 %collective-permute-done.76 = f32[2]{0:T(128)S(1)} collective-permute-done((f32[2]{0:T(128)S(1)}, f32[2]{0:T(128)S(1)}, u32[]{:S(2)}, u32[]{:S(2)}) %collective-permute-start.76) | collective-permute-done | bytes 40 | tf_op jit(solution)/shard_map/ppermute | solution.py:271
  433.2 5.8 %collective-permute-start.70 = (f32[4]{0:T(128)S(1)}, f32[4]{0:T(128)S(1)}, u32[]{:S(2)}, u32[]{:S(2)}) collective-permute-start(f32[4]{0:T(128)S(1)} %add.669), channel_id=1, source_target_pairs={{0,8},{4,12},{8,0},{12,4},{16,24},{20,28},{24,16},{28,20},{1,9},{5... | collective-permute-start | bytes 56 | tf_op jit(solution)/shard_map/ppermute | solution.py:271
  451.3 7.7 %shard_map.377 = (f32[18432,128]{1,0:T(8,128)}, f32[18432,128]{1,0:T(8,128)}, f32[18432,128]{1,0:T(8,128)}) custom-call(s32[1]{0:T(128)} %bitcast.29.where.refs_0_, f32[1]{0:T(128)S(6)} %mul.440.ratio.refs_1_, bf16[128,2304]{1,0:T(8,128)(2,1)} %maximum_select_fusion.5.part, bf16[128,2304]{1,0:T(8,128)(2,1)} %collective-permute-done.80.got, ...), custom_call_target="tpu_custom_call" | custom-call | bytes 14680064 | tf_op jit(solution)/shard_map/pallas_call | solution.py:89
  466.4 5.3 %collective-permute-done.72.refs_3_.got = bf16[544,512]{1,0:T(8,128)(2,1)S(1)} collective-permute-done((bf16[544,512]{1,0:T(8,128)(2,1)S(1)}, bf16[544,512]{1,0:T(8,128)(2,1)S(1)}, u32[]{:S(2)}, u32[]{:S(2)}) %collective-permute-start.72) | collective-permute-done | bytes 557088 | tf_op jit(solution)/shard_map/ppermute | solution.py:271
  473.4 7.4 %shard_map.378 = (f32[18432,128]{1,0:T(8,128)}, f32[18432,128]{1,0:T(8,128)}, f32[18432,128]{1,0:T(8,128)}) custom-call(s32[1]{0:T(128)} %bitcast.29.where.refs_0_, f32[1]{0:T(128)S(6)} %mul.440.ratio.refs_1_, bf16[128,2304]{1,0:T(8,128)(2,1)} %maximum_select_fusion.6.refs_2_, ...), custom_call_target="tpu_custom_call", output_to_operand_aliasing={{0}: (7, {}), {1}: (8, {}), {2}: (9, {})} | custom-call | bytes 14680064 | tf_op jit(solution)/shard_map/pallas_call | solution.py:89
  480.8 7.4 %shard_map.379 = (f32[18432,128]{1,0:T(8,128)}, f32[18432,128]{1,0:T(8,128)}, f32[18432,128]{1,0:T(8,128)}) custom-call(s32[1]{0:T(128)} %bitcast.39.where.refs_0_, f32[1]{0:T(128)S(6)} %mul.440.ratio.refs_1_, bf16[128,2304]{1,0:T(8,128)(2,1)} %maximum_select_fusion.7.refs_2_, ...), custom_call_target="tpu_custom_call", output_to_operand_aliasing={{0}: (7, {}), {1}: (8, {}), {2}: (9, {})} | custom-call | bytes 14680064 | tf_op jit(solution)/shard_map/pallas_call | solution.py:89
  489.4 7.7 %shard_map.380 = (f32[18432,128]{1,0:T(8,128)}, f32[18432,128]{1,0:T(8,128)}, f32[18432,128]{1,0:T(8,128)}) custom-call(s32[1]{0:T(128)} %bitcast.39.where.refs_0_, f32[1]{0:T(128)S(6)} %mul.440.ratio.refs_1_, bf16[128,2304]{1,0:T(8,128)(2,1)} %maximum_select_fusion.9.refs_2_, ...), custom_call_target="tpu_custom_call", output_to_operand_aliasing={{0}: (7, {}), {1}: (8, {}), {2}: (9, {})} | custom-call | bytes 14680064 | tf_op jit(solution)/shard_map/pallas_call | solution.py:89
  497.1 8.1 %shard_map.382 = (f32[2304,512]{1,0:T(8,128)}, f32[2304,512]{1,0:T(8,128)}, f32[2304,512]{1,0:T(8,128)}) custom-call(s32[1]{0:T(128)} %bitcast.29.where.refs_0_, f32[1]{0:T(128)S(6)} %mul.441.ratio.refs_1_, bf16[576,512]{1,0:T(8,128)(2,1)S(1)} %maximum_select_fusion.8.refs_2_, ...), custom_call_target="tpu_custom_call", output_to_operand_aliasing={{0}: (7, {}), {1}: (8, {}), {2}: (9, {})} | custom-call | bytes 14680064 | tf_op jit(solution)/shard_map/pallas_call | solution.py:89
  511.0 6.7 %shard_map.374 = (f32[1536,512]{1,0:T(8,128)}, f32[1536,512]{1,0:T(8,128)}, f32[1536,512]{1,0:T(8,128)}) custom-call(s32[1]{0:T(128)} %bitcast.29.where.refs_0_, f32[1]{0:T(128)S(6)} %mul.395.ratio.refs_1_, bf16[512,512]{1,0:T(8,128)(2,1)} %maximum_select_fusion.11.part, bf16[512,512]{1,0:T(8,128)(2,1)} %collective-permute-done.75.got, ...), custom_call_target="tpu_custom_call" | custom-call | bytes 13631488 | tf_op jit(solution)/shard_map/pallas_call | solution.py:89
  (509 shorter events, 283.1 us)
Async XLA Ops:
  45.3 42.2 %collective-permute-start.3 = (bf16[2,1040,512]{2,1,0:T(8,128)(2,1)}, bf16[2,1040,512]{2,1,0:T(8,128)(2,1)}, u32[]{:S(2)}, u32[]{:S(2)}) collective-permute-start(bf16[2,1040,512]{2,1,0:T(8,128)(2,1)} %pad_maximum_fusion.1), channel_id=1, source_target_pairs={{0,2},{3,1},{4,6},{7,5},{8,10},{11,9},{12,14},{15,13},{16,18},{19,... | collective-permute-start | bytes 6389768 | tf_op jit(solution)/shard_map/ppermute | solution.py:46
  70.7 38.1 %collective-permute-start.10 = (bf16[256,2304]{1,0:T(8,128)(2,1)S(1)}, bf16[256,2304]{1,0:T(8,128)(2,1)S(1)}, u32[]{:S(2)}, u32[]{:S(2)}) collective-permute-start(bf16[256,2304]{1,0:T(8,128)(2,1)S(1)} %maximum_select_fusion.1.g1), channel_id=1, source_target_pairs={{0,8},{4,12},{8,0},{12,4},{16,24},{20,28},{24,16},{28,20},{1,9},{5... | collective-permute-start | bytes 3538952 | tf_op jit(solution)/shard_map/ppermute | solution.py:271
  71.2 69.0 %collective-permute-start.15 = (bf16[2304,512]{1,0:T(8,128)(2,1)}, bf16[2304,512]{1,0:T(8,128)(2,1)}, u32[]{:S(2)}, u32[]{:S(2)}) collective-permute-start(bf16[2304,512]{1,0:T(8,128)(2,1)} %convert_element_type.453.d_own), channel_id=1, source_target_pairs={{0,1},{1,0},{2,3},{3,2},{4,5},{5,4},{6,7},{7,6},{8,9},{9,8},{10,11... | collective-permute-start | bytes 7077896 | tf_op jit(solution)/shard_map/ppermute | solution.py:34
  129.8 43.9 %collective-permute-start.14 = (bf16[1152,512]{1,0:T(8,128)(2,1)}, bf16[1152,512]{1,0:T(8,128)(2,1)}, u32[]{:S(2)}, u32[]{:S(2)}) collective-permute-start(bf16[1152,512]{1,0:T(8,128)(2,1)} %get-tuple-element.201), channel_id=1, source_target_pairs={{0,1},{1,0},{2,3},{3,2},{4,5},{5,4},{6,7},{7,6},{8,9},{9,8},{10,11... | collective-permute-start | bytes 3538952 | tf_op jit(solution)/shard_map/ppermute | solution.py:34
  137.6 59.4 %collective-permute-start.19 = (bf16[2,576,512]{2,1,0:T(8,128)(2,1)}, bf16[2,576,512]{2,1,0:T(8,128)(2,1)}, u32[]{:S(2)}, u32[]{:S(2)}) collective-permute-start(bf16[2,576,512]{2,1,0:T(8,128)(2,1)} %constant_dynamic-slice_fusion.2), channel_id=1, source_target_pairs={{0,4},{4,0},{8,12},{12,8},{16,20},{20,16},{24,28},{28,24},{1,5},{5... | collective-permute-start | bytes 3538952 | tf_op jit(solution)/shard_map/ppermute | solution.py:271
  168.5 30.2 %collective-permute-start.18 = (bf16[256,2304]{1,0:T(8,128)(2,1)}, bf16[256,2304]{1,0:T(8,128)(2,1)}, u32[]{:S(2)}, u32[]{:S(2)}) collective-permute-start(bf16[256,2304]{1,0:T(8,128)(2,1)} %get-tuple-element.213), channel_id=1, source_target_pairs={{0,1},{1,0},{2,3},{3,2},{4,5},{5,4},{6,7},{7,6},{8,9},{9,8},{10,11... | collective-permute-start | bytes 3538952 | tf_op jit(solution)/shard_map/ppermute | solution.py:34
  170.3 30.8 %collective-permute-start.17 = (bf16[2,128,2304]{2,1,0:T(8,128)(2,1)}, bf16[2,128,2304]{2,1,0:T(8,128)(2,1)}, u32[]{:S(2)}, u32[]{:S(2)}) collective-permute-start(bf16[2,128,2304]{2,1,0:T(8,128)(2,1)} %get-tuple-element.214), channel_id=1, source_target_pairs={{0,8},{4,12},{8,0},{12,4},{16,24},{20,28},{24,16},{28,20},{1,9},{5... | collective-permute-start | bytes 3538952 | tf_op jit(solution)/shard_map/ppermute | solution.py:271
  177.5 62.4 %collective-permute-start.27 = (bf16[256,2304]{1,0:T(8,128)(2,1)}, bf16[256,2304]{1,0:T(8,128)(2,1)}, u32[]{:S(2)}, u32[]{:S(2)}) collective-permute-start(bf16[256,2304]{1,0:T(8,128)(2,1)} %get-tuple-element.215), channel_id=1, source_target_pairs={{0,1},{1,0},{2,3},{3,2},{4,5},{5,4},{6,7},{7,6},{8,9},{9,8},{10,11... | collective-permute-start | bytes 3538952 | tf_op jit(solution)/shard_map/ppermute | solution.py:34
  179.2 23.6 %collective-permute-start.16 = (bf16[576,512]{1,0:T(8,128)(2,1)}, bf16[576,512]{1,0:T(8,128)(2,1)}, u32[]{:S(2)}, u32[]{:S(2)}) collective-permute-start(bf16[576,512]{1,0:T(8,128)(2,1)} %add_convert_fusion.7), channel_id=1, source_target_pairs={{0,4},{4,0},{8,12},{12,8},{16,20},{20,16},{24,28},{28,24},{1,5},{5... | collective-permute-start | bytes 1769480 | tf_op jit(solution)/shard_map/ppermute | solution.py:271
  196.9 28.0 %collective-permute-start.25 = (bf16[2,128,2304]{2,1,0:T(8,128)(2,1)}, bf16[2,128,2304]{2,1,0:T(8,128)(2,1)S(1)}, u32[]{:S(2)}, u32[]{:S(2)}) collective-permute-start(bf16[2,128,2304]{2,1,0:T(8,128)(2,1)} %get-tuple-element.222), channel_id=1, source_target_pairs={{0,8},{4,12},{8,0},{12,4},{16,24},{20,28},{24,16},{28,20},{1,9},{5... | collective-permute-start | bytes 3538952 | tf_op jit(solution)/shard_map/ppermute | solution.py:271
  200.0 36.8 %collective-permute-start.28 = (bf16[128,2304]{1,0:T(8,128)(2,1)S(1)}, bf16[128,2304]{1,0:T(8,128)(2,1)S(1)}, u32[]{:S(2)}, u32[]{:S(2)}) collective-permute-start(bf16[128,2304]{1,0:T(8,128)(2,1)S(1)} %add_convert_fusion.5), channel_id=1, source_target_pairs={{0,4},{4,0},{8,12},{12,8},{16,20},{20,16},{24,28},{28,24},{1,5},{5... | collective-permute-start | bytes 1769480 | tf_op jit(solution)/shard_map/ppermute | solution.py:271
  225.0 32.0 %collective-permute-start.30 = (bf16[1024,512]{1,0:T(8,128)(2,1)}, bf16[1024,512]{1,0:T(8,128)(2,1)}, u32[]{:S(2)}, u32[]{:S(2)}) collective-permute-start(bf16[1024,512]{1,0:T(8,128)(2,1)} %get-tuple-element.234), channel_id=1, source_target_pairs={{0,1},{1,0},{2,3},{3,2},{4,5},{5,4},{6,7},{7,6},{8,9},{9,8},{10,11... | collective-permute-start | bytes 3145736 | tf_op jit(solution)/shard_map/ppermute | solution.py:34
  227.6 24.1 %collective-permute-start.32 = (bf16[2,288,512]{2,1,0:T(8,128)(2,1)S(1)}, bf16[2,288,512]{2,1,0:T(8,128)(2,1)S(1)}, u32[]{:S(2)}, u32[]{:S(2)}) collective-permute-start(bf16[2,288,512]{2,1,0:T(8,128)(2,1)S(1)} %add_convert_fusion.6), channel_id=1, source_target_pairs={{0,8},{4,12},{8,0},{12,4},{16,24},{20,28},{24,16},{28,20},{1,9},{5... | collective-permute-start | bytes 1769480 | tf_op jit(solution)/shard_map/ppermute | solution.py:271
  239.9 38.8 %collective-permute-start.36 = (bf16[2,64,2304]{2,1,0:T(8,128)(2,1)}, bf16[2,64,2304]{2,1,0:T(8,128)(2,1)}, u32[]{:S(2)}, u32[]{:S(2)}) collective-permute-start(bf16[2,64,2304]{2,1,0:T(8,128)(2,1)} %add_convert_fusion.3), channel_id=1, source_target_pairs={{0,4},{4,0},{8,12},{12,8},{16,20},{20,16},{24,28},{28,24},{1,5},{5... | collective-permute-start | bytes 1769480 | tf_op jit(solution)/shard_map/ppermute | solution.py:271
  253.8 34.6 %collective-permute-start.26 = (bf16[1088,512]{1,0:T(8,128)(2,1)}, bf16[1088,512]{1,0:T(8,128)(2,1)}, u32[]{:S(2)}, u32[]{:S(2)}) collective-permute-start(bf16[1088,512]{1,0:T(8,128)(2,1)} %constant_dynamic-update-slice_fusion.4), channel_id=1, source_target_pairs={{0,1},{1,0},{2,3},{3,2},{4,5},{5,4},{6,7},{7,6},{8,9},{9,8},{10,11... | collective-permute-start | bytes 3342344 | tf_op jit(solution)/shard_map/ppermute | solution.py:34
  257.0 23.7 %collective-permute-start.35 = (bf16[288,512]{1,0:T(8,128)(2,1)S(1)}, bf16[288,512]{1,0:T(8,128)(2,1)S(1)}, u32[]{:S(2)}, u32[]{:S(2)}) collective-permute-start(bf16[288,512]{1,0:T(8,128)(2,1)S(1)} %add_convert_fusion.20), channel_id=1, source_target_pairs={{0,16},{4,20},{8,24},{12,28},{16,0},{20,4},{24,8},{28,12},{1,17},{... | collective-permute-start | bytes 884744 | tf_op jit(solution)/shard_map/ppermute | solution.py:271
  270.6 35.8 %collective-permute-start.40 = (bf16[288,512]{1,0:T(8,128)(2,1)}, bf16[288,512]{1,0:T(8,128)(2,1)S(1)}, u32[]{:S(2)}, u32[]{:S(2)}) collective-permute-start(bf16[288,512]{1,0:T(8,128)(2,1)} %fusion.33), channel_id=1, source_target_pairs={{0,1},{1,0},{2,3},{3,2},{4,5},{5,4},{6,7},{7,6},{8,9},{9,8},{10,11... | collective-permute-start | bytes 884744 | tf_op jit(solution)/shard_map/ppermute | solution.py:34
  277.3 24.5 %collective-permute-start.42 = (bf16[64,2304]{1,0:T(8,128)(2,1)}, bf16[64,2304]{1,0:T(8,128)(2,1)S(1)}, u32[]{:S(2)}, u32[]{:S(2)}) collective-permute-start(bf16[64,2304]{1,0:T(8,128)(2,1)} %fusion.32), channel_id=1, source_target_pairs={{0,1},{1,0},{2,3},{3,2},{4,5},{5,4},{6,7},{7,6},{8,9},{9,8},{10,11... | collective-permute-start | bytes 884744 | tf_op jit(solution)/shard_map/ppermute | solution.py:34
  294.0 38.2 %collective-permute-start.50 = (bf16[64,2304]{1,0:T(8,128)(2,1)}, bf16[64,2304]{1,0:T(8,128)(2,1)S(1)}, u32[]{:S(2)}, u32[]{:S(2)}) collective-permute-start(bf16[64,2304]{1,0:T(8,128)(2,1)} %fusion.34), channel_id=1, source_target_pairs={{0,1},{1,0},{2,3},{3,2},{4,5},{5,4},{6,7},{7,6},{8,9},{9,8},{10,11... | collective-permute-start | bytes 884744 | tf_op jit(solution)/shard_map/ppermute | solution.py:34
  301.8 23.6 %collective-permute-start.38 = (bf16[544,512]{1,0:T(8,128)(2,1)S(1)}, bf16[544,512]{1,0:T(8,128)(2,1)S(1)}, u32[]{:S(2)}, u32[]{:S(2)}) collective-permute-start(bf16[544,512]{1,0:T(8,128)(2,1)S(1)} %add_convert_fusion.8), channel_id=1, source_target_pairs={{0,4},{4,0},{8,12},{12,8},{16,20},{20,16},{24,28},{28,24},{1,5},{5... | collective-permute-start | bytes 1671176 | tf_op jit(solution)/shard_map/ppermute | solution.py:271
  303.2 45.1 %collective-permute-start.47 = (bf16[64,2304]{1,0:T(8,128)(2,1)S(1)}, bf16[64,2304]{1,0:T(8,128)(2,1)S(1)}, u32[]{:S(2)}, u32[]{:S(2)}) collective-permute-start(bf16[64,2304]{1,0:T(8,128)(2,1)S(1)} %fusion.9), channel_id=1, source_target_pairs={{0,16},{4,20},{8,24},{12,28},{16,0},{20,4},{24,8},{28,12},{1,17},{... | collective-permute-start | bytes 884744 | tf_op jit(solution)/shard_map/ppermute | solution.py:271
  306.4 37.8 %collective-permute-start.48 = (bf16[64,2304]{1,0:T(8,128)(2,1)S(1)}, bf16[64,2304]{1,0:T(8,128)(2,1)}, u32[]{:S(2)}, u32[]{:S(2)}) collective-permute-start(bf16[64,2304]{1,0:T(8,128)(2,1)S(1)} %add_convert_fusion.14.grad), channel_id=1, source_target_pairs={{0,8},{4,12},{8,0},{12,4},{16,24},{20,28},{24,16},{28,20},{1,9},{5... | collective-permute-start | bytes 884744 | tf_op jit(solution)/shard_map/ppermute | solution.py:271
  321.1 29.0 %collective-permute-start.46 = (bf16[288,512]{1,0:T(8,128)(2,1)S(1)}, bf16[288,512]{1,0:T(8,128)(2,1)S(1)}, u32[]{:S(2)}, u32[]{:S(2)}) collective-permute-start(bf16[288,512]{1,0:T(8,128)(2,1)S(1)} %fusion.10), channel_id=1, source_target_pairs={{0,16},{4,20},{8,24},{12,28},{16,0},{20,4},{24,8},{28,12},{1,17},{... | collective-permute-start | bytes 884744 | tf_op jit(solution)/shard_map/ppermute | solution.py:271
  332.3 32.1 %collective-permute-start.83 = (bf16[576,512]{1,0:T(8,128)(2,1)S(1)}, bf16[576,512]{1,0:T(8,128)(2,1)S(1)}, u32[]{:S(2)}, u32[]{:S(2)}) collective-permute-start(bf16[576,512]{1,0:T(8,128)(2,1)S(1)} %maximum_select_fusion.4.part), channel_id=1, source_target_pairs={{0,4},{4,0},{8,12},{12,8},{16,20},{20,16},{24,28},{28,24},{1,5},{5... | collective-permute-start | bytes 1769480 | tf_op jit(solution)/shard_map/ppermute | solution.py:271
  348.3 24.2 %collective-permute-start.54 = (bf16[64,2304]{1,0:T(8,128)(2,1)S(1)}, bf16[64,2304]{1,0:T(8,128)(2,1)S(1)}, u32[]{:S(2)}, u32[]{:S(2)}) collective-permute-start(bf16[64,2304]{1,0:T(8,128)(2,1)S(1)} %fusion.8), channel_id=1, source_target_pairs={{0,16},{4,20},{8,24},{12,28},{16,0},{20,4},{24,8},{28,12},{1,17},{... | collective-permute-start | bytes 884744 | tf_op jit(solution)/shard_map/ppermute | solution.py:271
  367.4 52.6 %collective-permute-start.79 = (bf16[128,2304]{1,0:T(8,128)(2,1)}, bf16[128,2304]{1,0:T(8,128)(2,1)}, u32[]{:S(2)}, u32[]{:S(2)}) collective-permute-start(bf16[128,2304]{1,0:T(8,128)(2,1)} %maximum_select_fusion.6.refs_2_), channel_id=1, source_target_pairs={{0,4},{4,0},{8,12},{12,8},{16,20},{20,16},{24,28},{28,24},{1,5},{5... | collective-permute-start | bytes 1769480 | tf_op jit(solution)/shard_map/ppermute | solution.py:271
  372.5 50.5 %collective-permute-start.80 = (bf16[128,2304]{1,0:T(8,128)(2,1)}, bf16[128,2304]{1,0:T(8,128)(2,1)}, u32[]{:S(2)}, u32[]{:S(2)}) collective-permute-start(bf16[128,2304]{1,0:T(8,128)(2,1)} %maximum_select_fusion.5.part), channel_id=1, source_target_pairs={{0,4},{4,0},{8,12},{12,8},{16,20},{20,16},{24,28},{28,24},{1,5},{5... | collective-permute-start | bytes 1769480 | tf_op jit(solution)/shard_map/ppermute | solution.py:271
  378.4 33.0 %collective-permute-start.65 = (bf16[64,2304]{1,0:T(8,128)(2,1)S(1)}, bf16[64,2304]{1,0:T(8,128)(2,1)}, u32[]{:S(2)}, u32[]{:S(2)}) collective-permute-start(bf16[64,2304]{1,0:T(8,128)(2,1)S(1)} %add_convert_fusion.10.grad), channel_id=1, source_target_pairs={{0,4},{4,0},{8,12},{12,8},{16,20},{20,16},{24,28},{28,24},{1,5},{5... | collective-permute-start | bytes 884744 | tf_op jit(solution)/shard_map/ppermute | solution.py:271
  387.1 71.8 %collective-permute-start.78 = (bf16[128,2304]{1,0:T(8,128)(2,1)}, bf16[128,2304]{1,0:T(8,128)(2,1)}, u32[]{:S(2)}, u32[]{:S(2)}) collective-permute-start(bf16[128,2304]{1,0:T(8,128)(2,1)} %maximum_select_fusion.7.refs_2_), channel_id=1, source_target_pairs={{0,8},{4,12},{8,0},{12,4},{16,24},{20,28},{24,16},{28,20},{1,9},{5... | collective-permute-start | bytes 1769480 | tf_op jit(solution)/shard_map/ppermute | solution.py:271
  415.4 49.1 %collective-permute-start.82 = (bf16[576,512]{1,0:T(8,128)(2,1)S(1)}, bf16[576,512]{1,0:T(8,128)(2,1)}, u32[]{:S(2)}, u32[]{:S(2)}) collective-permute-start(bf16[576,512]{1,0:T(8,128)(2,1)S(1)} %maximum_select_fusion.8.refs_2_), channel_id=1, source_target_pairs={{0,4},{4,0},{8,12},{12,8},{16,20},{20,16},{24,28},{28,24},{1,5},{5... | collective-permute-start | bytes 1769480 | tf_op jit(solution)/shard_map/ppermute | solution.py:271
  430.1 34.4 %collective-permute-start.75 = (bf16[512,512]{1,0:T(8,128)(2,1)}, bf16[512,512]{1,0:T(8,128)(2,1)}, u32[]{:S(2)}, u32[]{:S(2)}) collective-permute-start(bf16[512,512]{1,0:T(8,128)(2,1)} %maximum_select_fusion.11.part), channel_id=1, source_target_pairs={{0,4},{4,0},{8,12},{12,8},{16,20},{20,16},{24,28},{28,24},{1,5},{5... | collective-permute-start | bytes 1572872 | tf_op jit(solution)/shard_map/ppermute | solution.py:271
  440.6 23.9 %collective-permute-start.77 = (bf16[128,2304]{1,0:T(8,128)(2,1)}, bf16[128,2304]{1,0:T(8,128)(2,1)S(1)}, u32[]{:S(2)}, u32[]{:S(2)}) collective-permute-start(bf16[128,2304]{1,0:T(8,128)(2,1)} %maximum_select_fusion.9.refs_2_), channel_id=1, source_target_pairs={{0,8},{4,12},{8,0},{12,4},{16,24},{20,28},{24,16},{28,20},{1,9},{5... | collective-permute-start | bytes 1769480 | tf_op jit(solution)/shard_map/ppermute | solution.py:271
  (145 other events, 1588.7 us)
where the time goes:
time: 531 us; the launch traced here: 525 us
  Pallas kernels  151 us (28%)
  waiting for transfers between devices  123 us (23%)
  starting transfers between devices  106 us (20%)
  other arithmetic  81.3 us (15%)
  local copies, waits for them, and re-layouts  42.2 us (8%)
  between operations  11.9 us (2%)
  matrix products  8.95 us (2%)
    ppermute x52, waiting for transfers between devices, flip(): return lax.ppermute(values, 'dp', [(i, i ^ 1 << bit) for i in range(size)])  96.4 us
    pallas_call x17, Pallas kernels, kernel_call(): pl.pallas_call(kernel, grid_spec=pltpu.PrefetchScalarGridSpec(num_scalar_...  82.8 us
    pallas_call x10, Pallas kernels, local_call(): pl.pallas_call(kernel, grid_spec=pltpu.PrefetchScalarGridSpec(num_scalar_...  67.3 us
    ppermute x52, starting transfers between devices, flip(): return lax.ppermute(values, 'dp', [(i, i ^ 1 << bit) for i in range(size)])  62.8 us
    convert_element_type x32, other arithmetic, low_total(): return total_of(pieces).astype(low)  38.2 us
    unnamed x199, local copies, waits for them, and re-layouts  30.6 us
    ppermute x25, starting transfers between devices, swap(): return lax.ppermute(values, axis, [(0, 1), (1, 0)])  29.6 us
    select_n x12, other arithmetic, keep_or_join(): jnp.where(dp_bit(bit) == 0, jnp.concatenate([part, other]), jnp.concatena...  17.3 us
  transfers between devices with their start and end apart: 84, of which 27 were waited for; matrix products, arithmetic and copies ran while one was open for 19% of the time, Pallas kernels for 26%

commit v1 on v0

--- a/solution.py
+++ b/solution.py
@@ -341,8 +341,10 @@
     return part, got
 
 
-def norm_sum(values):
-    for step in ("x", "row", 1, 0):
+def norm_sum(values, steps, others=None):
+    for step in steps:
+        if step == 1 and others is not None:
+            values = jnp.concatenate([values, others()])
         got = yield step, values
         values = values + got
     return values
@@ -372,8 +374,8 @@
     def add(self, name, chunk, order):
         self.chunks[name] = chunk_sum(chunk, order, functools.partial(self.shares.__setitem__, name))
 
-    def add_norms(self, name, values):
-        self.chunks[name] = norm_sum(values)
+    def add_norms(self, name, values, steps=("x", "row", 1, 0), others=None):
+        self.chunks[name] = norm_sum(values, steps, others)
 
     def turn(self, name):
         got = self.arrivals.get(name)
@@ -961,13 +963,15 @@
         share_norms(wheres[n], shares[n], [(gu_state, 2 * k)], quarter // 2 * pairs, pairs=True)
         for k, n in enumerate("abce")
     )
-    turns.add_norms("n", gu_squares)
+    turns.add_norms("n", gu_squares, ("x", "row"))
     turns.run("nIdnbipn")
     turns.reach_shares("Ii")
     io_squares = share_norms(wheres["i"], shares["i"], [(in_state, 4), (out_state, 0)], part_rows)
     in_squares = share_norms(wheres["I"], shares["I"], [(in_state, 0)], part_rows)
-    turns.add_norms("m", io_squares + jnp.pad(in_squares, (0, 2)))
-    turns.run("mednIenimIimmm")
+    turns.add_norms(
+        "m", io_squares + jnp.pad(in_squares, (0, 2)), others=lambda: turns.done["n"]
+    )
+    turns.run("medmIemimIim")
     turns.finish()
     sums, seen = turns.done, turns.seen
 
@@ -991,8 +995,10 @@
         norms = jnp.sqrt(norms)
         return norms, (learn_rate * (norms[0] / (norms[1] + adam_eps))).reshape(1)
 
-    (gu_norms, gu_ratio), (down_norms, down_ratio) = [ratio_of(sums[name]) for name in "np"]
-    (in_norms, in_ratio), (out_norms, out_ratio) = [ratio_of(sums["m"][k : k + 2]) for k in (0, 2)]
+    down_norms, down_ratio = ratio_of(sums["p"])
+    (in_norms, in_ratio), (out_norms, out_ratio), (gu_norms, gu_ratio) = [
+        ratio_of(sums["m"][k : k + 2]) for k in (0, 2, 4)
+    ]
 
     def later_half(count):
         return functools.partial(lamb_plain, lambda i: (i >= count // 2).astype(jnp.int32))

time: 531 us -> 526 us (level)
  starting transfers between devices: 106 us -> 98.8 us
    ppermute x52 -> x50, starting transfers between devices: 62.8 us -> 54.3 us  [flip(): return lax.ppermute(values, 'dp', [(i, i ^ 1 << bit) for i in range(size)])]
    ppermute x52 -> x50, waiting for transfers between devices: 96.4 us -> 100 us  [flip(): return lax.ppermute(values, 'dp', [(i, i ^ 1 << bit) for i in range(size)])]
    unnamed x199 -> x209, local copies, waits for them, and re-layouts: 30.6 us -> 30.4 us
  transfers between devices with their start and end apart: 84 -> 82, of which waited for: 27 -> 26; matrix products, arithmetic and copies ran while one was open for 19% -> 19% of each run, Pallas kernels for 26% -> 27%
where the time goes in v1:
time: 526 us; the launch traced here: 519 us
  Pallas kernels  151 us (29%)
  waiting for transfers between devices  126 us (24%)
  starting transfers between devices  98.8 us (19%)
  other arithmetic  80.4 us (15%)
  local copies, waits for them, and re-layouts  42 us (8%)
  between operations  11.9 us (2%)
  matrix products  8.95 us (2%)
    ppermute x50, waiting for transfers between devices, flip(): return lax.ppermute(values, 'dp', [(i, i ^ 1 << bit) for i in range(size)])  100 us
    pallas_call x17, Pallas kernels, kernel_call(): pl.pallas_call(kernel, grid_spec=pltpu.PrefetchScalarGridSpec(num_scalar_...  82.6 us
    pallas_call x10, Pallas kernels, local_call(): pl.pallas_call(kernel, grid_spec=pltpu.PrefetchScalarGridSpec(num_scalar_...  67.2 us
    ppermute x50, starting transfers between devices, flip(): return lax.ppermute(values, 'dp', [(i, i ^ 1 << bit) for i in range(size)])  54.3 us
    convert_element_type x32, other arithmetic, low_total(): return total_of(pieces).astype(low)  38.2 us
    unnamed x209, local copies, waits for them, and re-layouts  30.4 us
    ppermute x25, starting transfers between devices, swap(): return lax.ppermute(values, axis, [(0, 1), (1, 0)])  29.4 us
    select_n x12, other arithmetic, keep_or_join(): jnp.where(dp_bit(bit) == 0, jnp.concatenate([part, other]), jnp.concatena...  17.4 us
  transfers between devices with their start and end apart: 82, of which 26 were waited for; matrix products, arithmetic and copies ran while one was open for 19% of the time, Pallas kernels for 27%

profile of v1, /device:TPU:0, one launch (start us, length us, event | category | flops | bytes accessed | tf_op | source)
XLA Modules:
  0.0 519.1 jit_solution(3224330752910348953)
XLA Ops:
  10.1 9.0 %collective-permute-done = bf16[512,512]{1,0:T(8,128)(2,1)} collective-permute-done((bf16[512,512]{1,0:T(8,128)(2,1)S(1)}, bf16[512,512]{1,0:T(8,128)(2,1)}, u32[]{:S(2)}, u32[]{:S(2)}) %collective-permute-start) | collective-permute-done | bytes 524320 | tf_op jit(solution)/shard_map/ppermute | solution.py:34
  33.7 8.8 %collective-permute-done.2 = bf16[1040,512]{1,0:T(8,128)(2,1)} collective-permute-done((bf16[1040,512]{1,0:T(8,128)(2,1)}, bf16[1040,512]{1,0:T(8,128)(2,1)}, u32[]{:S(2)}, u32[]{:S(2)}) %collective-permute-start.2) | collective-permute-done | bytes 1064992 | tf_op jit(solution)/shard_map/ppermute | solution.py:42
  55.4 4.2 convert_element_type.453.d_own
  61.0 5.8 %collective-permute-done.11 = bf16[128,2304]{1,0:T(8,128)(2,1)S(1)} collective-permute-done((bf16[128,2304]{1,0:T(8,128)(2,1)S(1)}, bf16[128,2304]{1,0:T(8,128)(2,1)S(1)}, u32[]{:S(2)}, u32[]{:S(2)}) %collective-permute-start.11) | collective-permute-done | bytes 589856 | tf_op jit(solution)/shard_map/ppermute | solution.py:34
  74.1 4.3 maximum_select_fusion.other
  78.4 8.2 %collective-permute-done.12 = bf16[128,2304]{1,0:T(8,128)(2,1)S(1)} collective-permute-done((bf16[128,2304]{1,0:T(8,128)(2,1)S(1)}, bf16[128,2304]{1,0:T(8,128)(2,1)S(1)}, u32[]{:S(2)}, u32[]{:S(2)}) %collective-permute-start.12) | collective-permute-done | bytes 589856 | tf_op jit(solution)/shard_map/ppermute | solution.py:271
  90.4 7.6 %shard_map.355 = (bf16[2,528,512]{2,1,0:T(8,128)(2,1)S(1)}, f32[528,512]{1,0:T(8,128)S(1)}, f32[528,512]{1,0:T(8,128)S(1)}, f32[528,512]{1,0:T(8,128)}, f32[512,...) custom-call(bf16[2,1040,512]{2,1,0:T(8,128)(2,1)} %copy-done.1, ...), custom_call_target="tpu_custom_call" | custom-call | bytes 1048576 | tf_op jit(solution)/shard_map/pallas_call | solution.py:445
  103.4 5.4 %collective-permute-done.10.g2 = bf16[256,2304]{1,0:T(8,128)(2,1)S(1)} collective-permute-done((bf16[256,2304]{1,0:T(8,128)(2,1)S(1)}, bf16[256,2304]{1,0:T(8,128)(2,1)S(1)}, u32[]{:S(2)}, u32[]{:S(2)}) %collective-permute-start.10) | collective-permute-done | bytes 1179680 | tf_op jit(solution)/shard_map/ppermute | solution.py:271
  111.0 13.6 %shard_map.357 = (bf16[2,512,512]{2,1,0:T(8,128)(2,1)S(1)}, f32[2,512,512]{2,1,0:T(8,128)}, f32[512,2304]{1,0:T(8,128)}, f32[512,2304]{1,0:T(8,128)}, bf16[512,2304]{1,0:T(8,128)(2,1)}) custom-call(s32[2]{0:T(128)S(1)} %pad_add_fusion.bits, bf16[2,1040,512]{2,1,0:T(8,128)(2,1)} %copy-done.1, bf16[512,512]{1,0:T(8,128)(2,1)S(1)} %get-tuple-element.188.mine0, ...), custom_call_target="tpu_custom_call" | custom-call | bytes 1048576 | tf_op jit(solution)/shard_map/pallas_call | solution.py:445
  124.6 4.1 shard_map.358
  140.2 16.1 %shard_map.360 = (bf16[512,2304]{1,0:T(8,128)(2,1)}, bf16[512,2304]{1,0:T(8,128)(2,1)}, bf16[512,512]{1,0:T(8,128)(2,1)S(1)}, bf16[512,512]{1,0:T(8,128)(2,1)S(1)}) custom-call(s32[2]{0:T(128)S(1)} %pad_add_fusion.bits, bf16[2,1040,512]{2,1,0:T(8,128)(2,1)} %copy-done.1, bf16[2304,512]{1,0:T(8,128)(2,1)} %convert_element_type.453.d_own, ...), custom_call_target="tpu_custom_call" | custom-call | bytes 1048576 | tf_op jit(solution)/shard_map/pallas_call | solution.py:445
  158.0 5.0 shard_map.361
  163.0 5.4 %shard_map.362 = (bf16[256,2304]{1,0:T(8,128)(2,1)S(1)}, bf16[256,2304]{1,0:T(8,128)(2,1)}, bf16[2,256,2304]{2,1,0:T(8,128)(2,1)S(1)}) custom-call(bf16[2,512,512]{2,1,0:T(8,128)(2,1)S(1)} %copy-done.28, bf16[512,2304]{1,0:T(8,128)(2,1)} %get-tuple-element.206.g_gate, bf16[512,2304]{1,0:T(8,128)(2,1)} %get-tuple-element.207.g_up), custom_call_target="tpu_custom_call" | custom-call | bytes 1048576 | tf_op jit(solution)/shard_map/pallas_call | solution.py:445
  180.9 7.2 %shard_map.363 = (f32[2,512,512]{2,1,0:T(8,128)}, bf16[2,512,512]{2,1,0:T(8,128)(2,1)S(1)}, bf16[3,528,512]{2,1,0:T(8,128)(2,1)}, f32[2,1,512]{2,1,0:T(1,128)S(1)}, f32[3,512]{1,0:T(4,128)S(1)}) custom-call(bf16[512,512]{1,0:T(8,128)(2,1)S(1)} %copy-done.57, bf16[512,512]{1,0:T(8,128)(2,1)S(1)} %copy-done.59, ...), custom_call_target="tpu_custom_call" | custom-call | bytes 1048576 | tf_op jit(solution)/shard_map/pallas_call | solution.py:445
  217.3 7.7 %collective-permute-done.25 = bf16[2,128,2304]{2,1,0:T(8,128)(2,1)S(1)} collective-permute-done((bf16[2,128,2304]{2,1,0:T(8,128)(2,1)}, bf16[2,128,2304]{2,1,0:T(8,128)(2,1)S(1)}, u32[]{:S(2)}, u32[]{:S(2)}) %collective-permute-start.25) | collective-permute-done | bytes 1179680 | tf_op jit(solution)/shard_map/ppermute | solution.py:271
  264.6 6.0 %collective-permute-done.29 = bf16[128,2304]{1,0:T(8,128)(2,1)} collective-permute-done((bf16[128,2304]{1,0:T(8,128)(2,1)}, bf16[128,2304]{1,0:T(8,128)(2,1)}, u32[]{:S(2)}, u32[]{:S(2)}) %collective-permute-start.29) | collective-permute-done | bytes 589856 | tf_op jit(solution)/shard_map/ppermute | solution.py:271
  272.3 4.8 collective-permute-done.37
  296.6 4.7 collective-permute-done.43
  310.6 10.0 %collective-permute-done.39 = bf16[64,2304]{1,0:T(8,128)(2,1)} collective-permute-done((bf16[64,2304]{1,0:T(8,128)(2,1)S(1)}, bf16[64,2304]{1,0:T(8,128)(2,1)}, u32[]{:S(2)}, u32[]{:S(2)}) %collective-permute-start.39) | collective-permute-done | bytes 294944 | tf_op jit(solution)/shard_map/ppermute | solution.py:271
  324.9 5.1 collective-permute-start.49
  333.0 9.5 %collective-permute-done.49 = bf16[256,512]{1,0:T(8,128)(2,1)S(1)} collective-permute-done((bf16[256,512]{1,0:T(8,128)(2,1)S(1)}, bf16[256,512]{1,0:T(8,128)(2,1)S(1)}, u32[]{:S(2)}, u32[]{:S(2)}) %collective-permute-start.49) | collective-permute-done | bytes 262176 | tf_op jit(solution)/shard_map/ppermute | solution.py:271
  352.5 5.7 %collective-permute-done.52 = bf16[64,2304]{1,0:T(8,128)(2,1)S(1)} collective-permute-done((bf16[64,2304]{1,0:T(8,128)(2,1)S(1)}, bf16[64,2304]{1,0:T(8,128)(2,1)S(1)}, u32[]{:S(2)}, u32[]{:S(2)}) %collective-permute-start.52) | collective-permute-done | bytes 294944 | tf_op jit(solution)/shard_map/ppermute | solution.py:271
  386.9 4.2 collective-permute-done.53
  402.8 7.7 %shard_map.381 = (f32[2304,512]{1,0:T(8,128)}, f32[2304,512]{1,0:T(8,128)}, f32[2304,512]{1,0:T(8,128)}) custom-call(s32[1]{0:T(128)} %bitcast.29.where.refs_0_, f32[1]{0:T(128)S(6)} %mul.441.ratio.refs_1_, bf16[576,512]{1,0:T(8,128)(2,1)S(1)} %copy-done.30, bf16[576,512]{1,0:T(8,128)(2,1)S(1)} %copy-done.51, f32[2304,512]{1,0:T(8,128)S(1)} %copy-done.5, ...), custom_call_target="tpu_custom_call" | custom-call | bytes 14680064 | tf_op jit(solution)/shard_map/pallas_call | solution.py:89
  424.1 6.8 %collective-permute-done.69 = f32[6]{0:T(128)S(1)} collective-permute-done((f32[6]{0:T(128)S(1)}, f32[6]{0:T(128)S(1)}, u32[]{:S(2)}, u32[]{:S(2)}) %collective-permute-start.69) | collective-permute-done | bytes 56 | tf_op jit(solution)/shard_map/ppermute | solution.py:271
  432.2 11.3 %collective-permute-done.70 = f32[6]{0:T(128)S(1)} collective-permute-done((f32[6]{0:T(128)S(1)}, f32[6]{0:T(128)S(1)}, u32[]{:S(2)}, u32[]{:S(2)}) %collective-permute-start.70) | collective-permute-done | bytes 56 | tf_op jit(solution)/shard_map/ppermute | solution.py:271
  458.7 7.7 %shard_map.377 = (f32[18432,128]{1,0:T(8,128)}, f32[18432,128]{1,0:T(8,128)}, f32[18432,128]{1,0:T(8,128)}) custom-call(s32[1]{0:T(128)} %bitcast.29.where.refs_0_, f32[1]{0:T(128)S(6)} %mul.440.ratio.refs_1_, bf16[128,2304]{1,0:T(8,128)(2,1)} %maximum_select_fusion.5.part, bf16[128,2304]{1,0:T(8,128)(2,1)} %collective-permute-done.78.got, ...), custom_call_target="tpu_custom_call" | custom-call | bytes 14680064 | tf_op jit(solution)/shard_map/pallas_call | solution.py:89
  469.2 7.5 %shard_map.378 = (f32[18432,128]{1,0:T(8,128)}, f32[18432,128]{1,0:T(8,128)}, f32[18432,128]{1,0:T(8,128)}) custom-call(s32[1]{0:T(128)} %bitcast.29.where.refs_0_, f32[1]{0:T(128)S(6)} %mul.440.ratio.refs_1_, bf16[128,2304]{1,0:T(8,128)(2,1)} %maximum_select_fusion.6.refs_2_, ...), custom_call_target="tpu_custom_call", output_to_operand_aliasing={{0}: (7, {}), {1}: (8, {}), {2}: (9, {})} | custom-call | bytes 14680064 | tf_op jit(solution)/shard_map/pallas_call | solution.py:89
  476.7 7.1 %shard_map.379 = (f32[18432,128]{1,0:T(8,128)}, f32[18432,128]{1,0:T(8,128)}, f32[18432,128]{1,0:T(8,128)}) custom-call(s32[1]{0:T(128)} %bitcast.39.where.refs_0_, f32[1]{0:T(128)S(6)} %mul.440.ratio.refs_1_, bf16[128,2304]{1,0:T(8,128)(2,1)S(1)} %copy-done.33, ...), custom_call_target="tpu_custom_call", output_to_operand_aliasing={{0}: (7, {}), {1}: (8, {}), {2}: (9, {})} | custom-call | bytes 14680064 | tf_op jit(solution)/shard_map/pallas_call | solution.py:89
  483.9 7.7 %shard_map.380 = (f32[18432,128]{1,0:T(8,128)}, f32[18432,128]{1,0:T(8,128)}, f32[18432,128]{1,0:T(8,128)}) custom-call(s32[1]{0:T(128)} %bitcast.39.where.refs_0_, f32[1]{0:T(128)S(6)} %mul.440.ratio.refs_1_, bf16[128,2304]{1,0:T(8,128)(2,1)} %maximum_select_fusion.9.refs_2_, ...), custom_call_target="tpu_custom_call", output_to_operand_aliasing={{0}: (7, {}), {1}: (8, {}), {2}: (9, {})} | custom-call | bytes 14680064 | tf_op jit(solution)/shard_map/pallas_call | solution.py:89
  491.7 8.1 %shard_map.382 = (f32[2304,512]{1,0:T(8,128)}, f32[2304,512]{1,0:T(8,128)}, f32[2304,512]{1,0:T(8,128)}) custom-call(s32[1]{0:T(128)} %bitcast.29.where.refs_0_, f32[1]{0:T(128)S(6)} %mul.441.ratio.refs_1_, bf16[576,512]{1,0:T(8,128)(2,1)S(1)} %maximum_select_fusion.8.refs_2_, ...), custom_call_target="tpu_custom_call", output_to_operand_aliasing={{0}: (7, {}), {1}: (8, {}), {2}: (9, {})} | custom-call | bytes 14680064 | tf_op jit(solution)/shard_map/pallas_call | solution.py:89
  505.6 6.7 %shard_map.374 = (f32[1536,512]{1,0:T(8,128)}, f32[1536,512]{1,0:T(8,128)}, f32[1536,512]{1,0:T(8,128)}) custom-call(s32[1]{0:T(128)} %bitcast.29.where.refs_0_, f32[1]{0:T(128)S(6)} %mul.395.ratio.refs_1_, bf16[512,512]{1,0:T(8,128)(2,1)} %maximum_select_fusion.11.part, bf16[512,512]{1,0:T(8,128)(2,1)} %collective-permute-done.74.got, ...), custom_call_target="tpu_custom_call" | custom-call | bytes 13631488 | tf_op jit(solution)/shard_map/pallas_call | solution.py:89
  (514 shorter events, 274.1 us)
Async XLA Ops:
  45.3 42.3 %collective-permute-start.3 = (bf16[2,1040,512]{2,1,0:T(8,128)(2,1)}, bf16[2,1040,512]{2,1,0:T(8,128)(2,1)}, u32[]{:S(2)}, u32[]{:S(2)}) collective-permute-start(bf16[2,1040,512]{2,1,0:T(8,128)(2,1)} %pad_maximum_fusion.1), channel_id=1, source_target_pairs={{0,2},{3,1},{4,6},{7,5},{8,10},{11,9},{12,14},{15,13},{16,18},{19,... | collective-permute-start | bytes 6389768 | tf_op jit(solution)/shard_map/ppermute | solution.py:46
  70.7 38.1 %collective-permute-start.10 = (bf16[256,2304]{1,0:T(8,128)(2,1)S(1)}, bf16[256,2304]{1,0:T(8,128)(2,1)S(1)}, u32[]{:S(2)}, u32[]{:S(2)}) collective-permute-start(bf16[256,2304]{1,0:T(8,128)(2,1)S(1)} %maximum_select_fusion.1.g1), channel_id=1, source_target_pairs={{0,8},{4,12},{8,0},{12,4},{16,24},{20,28},{24,16},{28,20},{1,9},{5... | collective-permute-start | bytes 3538952 | tf_op jit(solution)/shard_map/ppermute | solution.py:271
  71.2 69.0 %collective-permute-start.15 = (bf16[2304,512]{1,0:T(8,128)(2,1)}, bf16[2304,512]{1,0:T(8,128)(2,1)}, u32[]{:S(2)}, u32[]{:S(2)}) collective-permute-start(bf16[2304,512]{1,0:T(8,128)(2,1)} %convert_element_type.453.d_own), channel_id=1, source_target_pairs={{0,1},{1,0},{2,3},{3,2},{4,5},{5,4},{6,7},{7,6},{8,9},{9,8},{10,11... | collective-permute-start | bytes 7077896 | tf_op jit(solution)/shard_map/ppermute | solution.py:34
  129.8 43.9 %collective-permute-start.14 = (bf16[1152,512]{1,0:T(8,128)(2,1)}, bf16[1152,512]{1,0:T(8,128)(2,1)}, u32[]{:S(2)}, u32[]{:S(2)}) collective-permute-start(bf16[1152,512]{1,0:T(8,128)(2,1)} %get-tuple-element.199), channel_id=1, source_target_pairs={{0,1},{1,0},{2,3},{3,2},{4,5},{5,4},{6,7},{7,6},{8,9},{9,8},{10,11... | collective-permute-start | bytes 3538952 | tf_op jit(solution)/shard_map/ppermute | solution.py:34
  137.6 59.4 %collective-permute-start.19 = (bf16[2,576,512]{2,1,0:T(8,128)(2,1)}, bf16[2,576,512]{2,1,0:T(8,128)(2,1)}, u32[]{:S(2)}, u32[]{:S(2)}) collective-permute-start(bf16[2,576,512]{2,1,0:T(8,128)(2,1)} %constant_dynamic-slice_fusion.2), channel_id=1, source_target_pairs={{0,4},{4,0},{8,12},{12,8},{16,20},{20,16},{24,28},{28,24},{1,5},{5... | collective-permute-start | bytes 3538952 | tf_op jit(solution)/shard_map/ppermute | solution.py:271
  168.5 30.2 %collective-permute-start.18 = (bf16[256,2304]{1,0:T(8,128)(2,1)}, bf16[256,2304]{1,0:T(8,128)(2,1)}, u32[]{:S(2)}, u32[]{:S(2)}) collective-permute-start(bf16[256,2304]{1,0:T(8,128)(2,1)} %get-tuple-element.211), channel_id=1, source_target_pairs={{0,1},{1,0},{2,3},{3,2},{4,5},{5,4},{6,7},{7,6},{8,9},{9,8},{10,11... | collective-permute-start | bytes 3538952 | tf_op jit(solution)/shard_map/ppermute | solution.py:34
  170.2 30.8 %collective-permute-start.17 = (bf16[2,128,2304]{2,1,0:T(8,128)(2,1)}, bf16[2,128,2304]{2,1,0:T(8,128)(2,1)}, u32[]{:S(2)}, u32[]{:S(2)}) collective-permute-start(bf16[2,128,2304]{2,1,0:T(8,128)(2,1)} %get-tuple-element.212), channel_id=1, source_target_pairs={{0,8},{4,12},{8,0},{12,4},{16,24},{20,28},{24,16},{28,20},{1,9},{5... | collective-permute-start | bytes 3538952 | tf_op jit(solution)/shard_map/ppermute | solution.py:271
  177.5 62.3 %collective-permute-start.27 = (bf16[256,2304]{1,0:T(8,128)(2,1)}, bf16[256,2304]{1,0:T(8,128)(2,1)}, u32[]{:S(2)}, u32[]{:S(2)}) collective-permute-start(bf16[256,2304]{1,0:T(8,128)(2,1)} %get-tuple-element.213), channel_id=1, source_target_pairs={{0,1},{1,0},{2,3},{3,2},{4,5},{5,4},{6,7},{7,6},{8,9},{9,8},{10,11... | collective-permute-start | bytes 3538952 | tf_op jit(solution)/shard_map/ppermute | solution.py:34
  179.2 23.6 %collective-permute-start.16 = (bf16[576,512]{1,0:T(8,128)(2,1)}, bf16[576,512]{1,0:T(8,128)(2,1)}, u32[]{:S(2)}, u32[]{:S(2)}) collective-permute-start(bf16[576,512]{1,0:T(8,128)(2,1)} %add_convert_fusion.7), channel_id=1, source_target_pairs={{0,4},{4,0},{8,12},{12,8},{16,20},{20,16},{24,28},{28,24},{1,5},{5... | collective-permute-start | bytes 1769480 | tf_op jit(solution)/shard_map/ppermute | solution.py:271
  196.9 28.0 %collective-permute-start.25 = (bf16[2,128,2304]{2,1,0:T(8,128)(2,1)}, bf16[2,128,2304]{2,1,0:T(8,128)(2,1)S(1)}, u32[]{:S(2)}, u32[]{:S(2)}) collective-permute-start(bf16[2,128,2304]{2,1,0:T(8,128)(2,1)} %get-tuple-element.220), channel_id=1, source_target_pairs={{0,8},{4,12},{8,0},{12,4},{16,24},{20,28},{24,16},{28,20},{1,9},{5... | collective-permute-start | bytes 3538952 | tf_op jit(solution)/shard_map/ppermute | solution.py:271
  200.0 36.7 %collective-permute-start.28 = (bf16[128,2304]{1,0:T(8,128)(2,1)S(1)}, bf16[128,2304]{1,0:T(8,128)(2,1)S(1)}, u32[]{:S(2)}, u32[]{:S(2)}) collective-permute-start(bf16[128,2304]{1,0:T(8,128)(2,1)S(1)} %add_convert_fusion.5), channel_id=1, source_target_pairs={{0,4},{4,0},{8,12},{12,8},{16,20},{20,16},{24,28},{28,24},{1,5},{5... | collective-permute-start | bytes 1769480 | tf_op jit(solution)/shard_map/ppermute | solution.py:271
  225.0 31.9 %collective-permute-start.30 = (bf16[1024,512]{1,0:T(8,128)(2,1)}, bf16[1024,512]{1,0:T(8,128)(2,1)}, u32[]{:S(2)}, u32[]{:S(2)}) collective-permute-start(bf16[1024,512]{1,0:T(8,128)(2,1)} %get-tuple-element.232), channel_id=1, source_target_pairs={{0,1},{1,0},{2,3},{3,2},{4,5},{5,4},{6,7},{7,6},{8,9},{9,8},{10,11... | collective-permute-start | bytes 3145736 | tf_op jit(solution)/shard_map/ppermute | solution.py:34
  227.5 24.1 %collective-permute-start.32 = (bf16[2,288,512]{2,1,0:T(8,128)(2,1)S(1)}, bf16[2,288,512]{2,1,0:T(8,128)(2,1)S(1)}, u32[]{:S(2)}, u32[]{:S(2)}) collective-permute-start(bf16[2,288,512]{2,1,0:T(8,128)(2,1)S(1)} %add_convert_fusion.6), channel_id=1, source_target_pairs={{0,8},{4,12},{8,0},{12,4},{16,24},{20,28},{24,16},{28,20},{1,9},{5... | collective-permute-start | bytes 1769480 | tf_op jit(solution)/shard_map/ppermute | solution.py:271
  239.9 38.7 %collective-permute-start.36 = (bf16[2,64,2304]{2,1,0:T(8,128)(2,1)}, bf16[2,64,2304]{2,1,0:T(8,128)(2,1)}, u32[]{:S(2)}, u32[]{:S(2)}) collective-permute-start(bf16[2,64,2304]{2,1,0:T(8,128)(2,1)} %add_convert_fusion.3), channel_id=1, source_target_pairs={{0,4},{4,0},{8,12},{12,8},{16,20},{20,16},{24,28},{28,24},{1,5},{5... | collective-permute-start | bytes 1769480 | tf_op jit(solution)/shard_map/ppermute | solution.py:271
  251.6 36.4 %collective-permute-start.26 = (bf16[1088,512]{1,0:T(8,128)(2,1)}, bf16[1088,512]{1,0:T(8,128)(2,1)}, u32[]{:S(2)}, u32[]{:S(2)}) collective-permute-start(bf16[1088,512]{1,0:T(8,128)(2,1)} %constant_dynamic-update-slice_fusion.4), channel_id=1, source_target_pairs={{0,1},{1,0},{2,3},{3,2},{4,5},{5,4},{6,7},{7,6},{8,9},{9,8},{10,11... | collective-permute-start | bytes 3342344 | tf_op jit(solution)/shard_map/ppermute | solution.py:34
  256.9 23.6 %collective-permute-start.35 = (bf16[288,512]{1,0:T(8,128)(2,1)S(1)}, bf16[288,512]{1,0:T(8,128)(2,1)S(1)}, u32[]{:S(2)}, u32[]{:S(2)}) collective-permute-start(bf16[288,512]{1,0:T(8,128)(2,1)S(1)} %add_convert_fusion.20), channel_id=1, source_target_pairs={{0,16},{4,20},{8,24},{12,28},{16,0},{20,4},{24,8},{28,12},{1,17},{... | collective-permute-start | bytes 884744 | tf_op jit(solution)/shard_map/ppermute | solution.py:271
  270.6 35.4 %collective-permute-start.40 = (bf16[288,512]{1,0:T(8,128)(2,1)}, bf16[288,512]{1,0:T(8,128)(2,1)S(1)}, u32[]{:S(2)}, u32[]{:S(2)}) collective-permute-start(bf16[288,512]{1,0:T(8,128)(2,1)} %fusion.33), channel_id=1, source_target_pairs={{0,1},{1,0},{2,3},{3,2},{4,5},{5,4},{6,7},{7,6},{8,9},{9,8},{10,11... | collective-permute-start | bytes 884744 | tf_op jit(solution)/shard_map/ppermute | solution.py:34
  277.1 24.3 %collective-permute-start.42 = (bf16[64,2304]{1,0:T(8,128)(2,1)}, bf16[64,2304]{1,0:T(8,128)(2,1)S(1)}, u32[]{:S(2)}, u32[]{:S(2)}) collective-permute-start(bf16[64,2304]{1,0:T(8,128)(2,1)} %fusion.32), channel_id=1, source_target_pairs={{0,1},{1,0},{2,3},{3,2},{4,5},{5,4},{6,7},{7,6},{8,9},{9,8},{10,11... | collective-permute-start | bytes 884744 | tf_op jit(solution)/shard_map/ppermute | solution.py:34
  293.7 38.1 %collective-permute-start.50 = (bf16[64,2304]{1,0:T(8,128)(2,1)}, bf16[64,2304]{1,0:T(8,128)(2,1)S(1)}, u32[]{:S(2)}, u32[]{:S(2)}) collective-permute-start(bf16[64,2304]{1,0:T(8,128)(2,1)} %fusion.34), channel_id=1, source_target_pairs={{0,1},{1,0},{2,3},{3,2},{4,5},{5,4},{6,7},{7,6},{8,9},{9,8},{10,11... | collective-permute-start | bytes 884744 | tf_op jit(solution)/shard_map/ppermute | solution.py:34
  302.7 45.0 %collective-permute-start.47 = (bf16[64,2304]{1,0:T(8,128)(2,1)S(1)}, bf16[64,2304]{1,0:T(8,128)(2,1)S(1)}, u32[]{:S(2)}, u32[]{:S(2)}) collective-permute-start(bf16[64,2304]{1,0:T(8,128)(2,1)S(1)} %fusion.9), channel_id=1, source_target_pairs={{0,16},{4,20},{8,24},{12,28},{16,0},{20,4},{24,8},{28,12},{1,17},{... | collective-permute-start | bytes 884744 | tf_op jit(solution)/shard_map/ppermute | solution.py:271
  305.9 37.7 %collective-permute-start.48 = (bf16[64,2304]{1,0:T(8,128)(2,1)S(1)}, bf16[64,2304]{1,0:T(8,128)(2,1)}, u32[]{:S(2)}, u32[]{:S(2)}) collective-permute-start(bf16[64,2304]{1,0:T(8,128)(2,1)S(1)} %add_convert_fusion.14.grad), channel_id=1, source_target_pairs={{0,8},{4,12},{8,0},{12,4},{16,24},{20,28},{24,16},{28,20},{1,9},{5... | collective-permute-start | bytes 884744 | tf_op jit(solution)/shard_map/ppermute | solution.py:271
  320.6 29.0 %collective-permute-start.46 = (bf16[288,512]{1,0:T(8,128)(2,1)S(1)}, bf16[288,512]{1,0:T(8,128)(2,1)S(1)}, u32[]{:S(2)}, u32[]{:S(2)}) collective-permute-start(bf16[288,512]{1,0:T(8,128)(2,1)S(1)} %fusion.10), channel_id=1, source_target_pairs={{0,16},{4,20},{8,24},{12,28},{16,0},{20,4},{24,8},{28,12},{1,17},{... | collective-permute-start | bytes 884744 | tf_op jit(solution)/shard_map/ppermute | solution.py:271
  331.8 32.5 %collective-permute-start.81 = (bf16[576,512]{1,0:T(8,128)(2,1)S(1)}, bf16[576,512]{1,0:T(8,128)(2,1)S(1)}, u32[]{:S(2)}, u32[]{:S(2)}) collective-permute-start(bf16[576,512]{1,0:T(8,128)(2,1)S(1)} %maximum_select_fusion.4.part), channel_id=1, source_target_pairs={{0,4},{4,0},{8,12},{12,8},{16,20},{20,16},{24,28},{28,24},{1,5},{5... | collective-permute-start | bytes 1769480 | tf_op jit(solution)/shard_map/ppermute | solution.py:271
  347.7 23.9 %collective-permute-start.54 = (bf16[64,2304]{1,0:T(8,128)(2,1)S(1)}, bf16[64,2304]{1,0:T(8,128)(2,1)S(1)}, u32[]{:S(2)}, u32[]{:S(2)}) collective-permute-start(bf16[64,2304]{1,0:T(8,128)(2,1)S(1)} %fusion.8), channel_id=1, source_target_pairs={{0,16},{4,20},{8,24},{12,28},{16,0},{20,4},{24,8},{28,12},{1,17},{... | collective-permute-start | bytes 884744 | tf_op jit(solution)/shard_map/ppermute | solution.py:271
  367.0 54.2 %collective-permute-start.77 = (bf16[128,2304]{1,0:T(8,128)(2,1)}, bf16[128,2304]{1,0:T(8,128)(2,1)}, u32[]{:S(2)}, u32[]{:S(2)}) collective-permute-start(bf16[128,2304]{1,0:T(8,128)(2,1)} %maximum_select_fusion.6.refs_2_), channel_id=1, source_target_pairs={{0,4},{4,0},{8,12},{12,8},{16,20},{20,16},{24,28},{28,24},{1,5},{5... | collective-permute-start | bytes 1769480 | tf_op jit(solution)/shard_map/ppermute | solution.py:271
  371.6 49.6 %collective-permute-start.78 = (bf16[128,2304]{1,0:T(8,128)(2,1)}, bf16[128,2304]{1,0:T(8,128)(2,1)}, u32[]{:S(2)}, u32[]{:S(2)}) collective-permute-start(bf16[128,2304]{1,0:T(8,128)(2,1)} %maximum_select_fusion.5.part), channel_id=1, source_target_pairs={{0,4},{4,0},{8,12},{12,8},{16,20},{20,16},{24,28},{28,24},{1,5},{5... | collective-permute-start | bytes 1769480 | tf_op jit(solution)/shard_map/ppermute | solution.py:271
  377.6 32.9 %collective-permute-start.63 = (bf16[64,2304]{1,0:T(8,128)(2,1)S(1)}, bf16[64,2304]{1,0:T(8,128)(2,1)}, u32[]{:S(2)}, u32[]{:S(2)}) collective-permute-start(bf16[64,2304]{1,0:T(8,128)(2,1)S(1)} %add_convert_fusion.10.grad), channel_id=1, source_target_pairs={{0,4},{4,0},{8,12},{12,8},{16,20},{20,16},{24,28},{28,24},{1,5},{5... | collective-permute-start | bytes 884744 | tf_op jit(solution)/shard_map/ppermute | solution.py:271
  386.8 31.1 %collective-permute-start.65 = (bf16[256,512]{1,0:T(8,128)(2,1)}, bf16[256,512]{1,0:T(8,128)(2,1)S(1)}, u32[]{:S(2)}, u32[]{:S(2)}) collective-permute-start(bf16[256,512]{1,0:T(8,128)(2,1)} %add_convert_fusion.28.grad), channel_id=1, source_target_pairs={{0,8},{4,12},{8,0},{12,4},{16,24},{20,28},{24,16},{28,20},{1,9},{5... | collective-permute-start | bytes 786440 | tf_op jit(solution)/shard_map/ppermute | solution.py:271
  397.3 25.2 %collective-permute-start.61 = (bf16[272,512]{1,0:T(8,128)(2,1)S(1)}, bf16[272,512]{1,0:T(8,128)(2,1)S(1)}, u32[]{:S(2)}, u32[]{:S(2)}) collective-permute-start(bf16[272,512]{1,0:T(8,128)(2,1)S(1)} %add_convert_fusion.25.grad), channel_id=1, source_target_pairs={{0,8},{4,12},{8,0},{12,4},{16,24},{20,28},{24,16},{28,20},{1,9},{5... | collective-permute-start | bytes 835592 | tf_op jit(solution)/shard_map/ppermute | solution.py:271
  415.8 34.8 %collective-permute-start.76 = (bf16[128,2304]{1,0:T(8,128)(2,1)S(1)}, bf16[128,2304]{1,0:T(8,128)(2,1)S(1)}, u32[]{:S(2)}, u32[]{:S(2)}) collective-permute-start(bf16[128,2304]{1,0:T(8,128)(2,1)S(1)} %copy-done.32), channel_id=1, source_target_pairs={{0,8},{4,12},{8,0},{12,4},{16,24},{20,28},{24,16},{28,20},{1,9},{5... | collective-permute-start | bytes 1769480 | tf_op jit(solution)/shard_map/ppermute | solution.py:271
  417.9 48.6 %collective-permute-start.80 = (bf16[576,512]{1,0:T(8,128)(2,1)S(1)}, bf16[576,512]{1,0:T(8,128)(2,1)}, u32[]{:S(2)}, u32[]{:S(2)}) collective-permute-start(bf16[576,512]{1,0:T(8,128)(2,1)S(1)} %maximum_select_fusion.8.refs_2_), channel_id=1, source_target_pairs={{0,4},{4,0},{8,12},{12,8},{16,20},{20,16},{24,28},{28,24},{1,5},{5... | collective-permute-start | bytes 1769480 | tf_op jit(solution)/shard_map/ppermute | solution.py:271
  421.3 45.2 %collective-permute-start.74 = (bf16[512,512]{1,0:T(8,128)(2,1)}, bf16[512,512]{1,0:T(8,128)(2,1)}, u32[]{:S(2)}, u32[]{:S(2)}) collective-permute-start(bf16[512,512]{1,0:T(8,128)(2,1)} %maximum_select_fusion.11.part), channel_id=1, source_target_pairs={{0,4},{4,0},{8,12},{12,8},{16,20},{20,16},{24,28},{28,24},{1,5},{5... | collective-permute-start | bytes 1572872 | tf_op jit(solution)/shard_map/ppermute | solution.py:271
  (148 other events, 1592.4 us)
